TPU v7x, 128 devices: a whole 4x4x4 slice. The times are simulated.
128 devices in a mesh: section: 2 (over y_lo), dp: 64 (over y_hi, z, x, core).
Axes of the slice: x: 4, y: 4 (y_hi: 2, y_lo: 2; y = y_hi * 2 + y_lo), z: 4, core: 2. Of those that a mesh axis runs over, the one named last changes fastest.
Arguments:
- tokens: bfloat16 [32768, 768], P('dp'), may hold values from -6 to 6
- segment_ids: int32 [32768], P('dp'), may hold values from 0 to 255, never falling along the last dimension, each value on 1 to 256 neighbouring positions
- depth: int32 [64], P('dp'), may hold values from 6 to 12, as said below
- input_weight: float32 [2, 768, 2304], P('section', 'dp'), may hold values from -0.21875 to 0.21875
- input_bias: float32 [2, 1536], P('section', 'dp'), may hold values from -3 to 3
- output_weight: float32 [2, 768, 768], P('section', 'dp'), may hold values from -0.625 to 0.625
- output_bias: float32 [2, 768], P('section', 'dp'), may hold values from -3 to 3
- first_gain: float32 [2, 768], P('section', 'dp'), may hold values from 0.5 to 1.5
- first_shift: float32 [2, 768], P('section', 'dp'), may hold values from -3 to 3
- expand_weight: float32 [2, 768, 3072], P('section', 'dp'), may hold values from -0.21875 to 0.21875
- expand_bias: float32 [2, 3072], P('section', 'dp'), may hold values from -3 to 3
- contract_weight: float32 [2, 3072, 768], P('section', 'dp'), may hold values from -0.15625 to 0.15625
- contract_bias: float32 [2, 768], P('section', 'dp'), may hold values from -3 to 3
- second_gain: float32 [2, 768], P('section', 'dp'), may hold values from 0.5 to 1.5
- second_shift: float32 [2, 768], P('section', 'dp'), may hold values from -3 to 3
- cotangent: bfloat16 [32768, 768], P('dp'), may hold values from -6 to 6
Outputs:
- layer_outputs: bfloat16 [2, 32768, 768], P('section', 'dp')
- input_grads: bfloat16 [2, 32768, 768], P('section', 'dp')
- input_weight_grad: float32 [2, 768, 2304], P('section', 'dp')
- input_bias_grad: float32 [2, 1536], P('section', 'dp')
- output_weight_grad: float32 [2, 768, 768], P('section', 'dp')
- output_bias_grad: float32 [2, 768], P('section', 'dp')
- first_gain_grad: float32 [2, 768], P('section', 'dp')
- first_shift_grad: float32 [2, 768], P('section', 'dp')
- expand_weight_grad: float32 [2, 768, 3072], P('section', 'dp')
- expand_bias_grad: float32 [2, 3072], P('section', 'dp')
- contract_weight_grad: float32 [2, 3072, 768], P('section', 'dp')
- contract_bias_grad: float32 [2, 768], P('section', 'dp')
- second_gain_grad: float32 [2, 768], P('section', 'dp')
- second_shift_grad: float32 [2, 768], P('section', 'dp')
Inputs may be any that keep to these rules, and one draw needn't show every extreme that they name: Each group's depth is 6, 9 or 12; some group has 12 and some has 6.
All inputs are finite; a program needn't handle non-finite values.
Results may differ from a plain program's by a relative error of at most 0.014.
Values may be sent and summed in bfloat16 or wider, within the bound.
No kernel may reach another device: no remote copies, remote signals or barrier semaphores. Data moves between devices by JAX's collectives and lax.ppermute only.
A program may use at most 384 MiB of HBM per device.

v0:
```python
import jax
import jax.numpy as jnp
from jax import lax
from jax.sharding import PartitionSpec as P

D = 768
HEADS = 12
MICRO = 2


epsilon = 1e-05


def shifted(value, axis, steps):
    count = lax.axis_size(axis)
    first, last = (max(0, -steps), min(count, count - steps))
    return lax.ppermute(value, axis, [(source, source + steps) for source in range(first, last)])


def norm_stats(residual):
    centre = residual - jnp.mean(residual, axis=1, keepdims=True)
    scaled = lax.rsqrt(jnp.mean(centre * centre, axis=1, keepdims=True) + epsilon)
    return (centre * scaled, scaled)


def norm_back(grad_out, normed, scaled, gain_row):
    grad_normed = grad_out * gain_row
    inner_term = (
        grad_normed
        - jnp.mean(grad_normed, axis=1, keepdims=True)
        - normed * jnp.mean(grad_normed * normed, axis=1, keepdims=True)
    )
    return (scaled * inner_term, jnp.sum(grad_out * normed, axis=0), jnp.sum(grad_out, axis=0))


def gelu_slope(pre_act):
    return (
        0.5 * (1.0 + lax.erf(pre_act * 0.7071067811865476))
        + pre_act * jnp.exp(-0.5 * pre_act * pre_act) * 0.3989422804014327
    )


def weight_grad(left, right):
    return jnp.einsum("rk,rn->kn", left, right, preferred_element_type=jnp.float32)


def back_product(left, right):
    return jnp.einsum("rn,kn->rk", left, right, preferred_element_type=jnp.float32)


def column_sums(values_low):
    return jnp.sum(values_low.astype(jnp.float32), axis=0)


def forward_parts(inputs_block, block_segments, weights):
    (
        input_weight,
        input_bias,
        output_weight,
        output_bias,
        first_gain,
        first_shift,
        expand_weight,
        expand_bias,
        contract_weight,
        contract_bias,
        second_gain,
        second_shift,
    ) = weights
    row_count, model_width = inputs_block.shape
    head_size = model_width // HEADS
    score_scale = head_size ** (-0.5)
    full_bias = jnp.concatenate(
        [
            input_bias[:model_width],
            jnp.zeros((model_width,), input_bias.dtype),
            input_bias[model_width:],
        ]
    ).astype(jnp.float32)
    projected = (
        jnp.dot(inputs_block, input_weight, preferred_element_type=jnp.float32) + full_bias
    ).astype(jnp.bfloat16)
    queries = projected[:, :model_width].reshape(row_count, HEADS, head_size)
    keys_part = projected[:, model_width : 2 * model_width].reshape(row_count, HEADS, head_size)
    values_part = projected[:, 2 * model_width :].reshape(row_count, HEADS, head_size)
    scores = (
        jnp.einsum("qhd,khd->hqk", queries, keys_part, preferred_element_type=jnp.float32)
        * score_scale
    )
    same_doc = block_segments[:, None] == block_segments[None, :]
    scores = jnp.where(same_doc[None], scores, -1e30)
    row_max = jnp.max(scores, axis=2, keepdims=True)
    exponent = jnp.exp(scores - row_max)
    softmax_rows = exponent / jnp.sum(exponent, axis=2, keepdims=True)
    softmax_low = softmax_rows.astype(jnp.bfloat16)
    attended = (
        jnp.einsum("hqk,khd->qhd", softmax_low, values_part, preferred_element_type=jnp.float32)
        .reshape(row_count, model_width)
        .astype(jnp.bfloat16)
    )
    branch = jnp.dot(
        attended, output_weight, preferred_element_type=jnp.float32
    ) + output_bias.astype(jnp.float32)
    normed_one, scaled_one = norm_stats(inputs_block.astype(jnp.float32) + branch)
    hidden = (normed_one * first_gain.astype(jnp.float32) + first_shift.astype(jnp.float32)).astype(
        jnp.bfloat16
    )
    pre_act = jnp.dot(
        hidden, expand_weight, preferred_element_type=jnp.float32
    ) + expand_bias.astype(jnp.float32)
    activated = jax.nn.gelu(pre_act, approximate=False).astype(jnp.bfloat16)
    ffn_out = jnp.dot(
        activated, contract_weight, preferred_element_type=jnp.float32
    ) + contract_bias.astype(jnp.float32)
    normed_two, scaled_two = norm_stats(hidden.astype(jnp.float32) + ffn_out)
    result = normed_two * second_gain.astype(jnp.float32) + second_shift.astype(jnp.float32)
    saved = (
        queries,
        keys_part,
        values_part,
        softmax_rows,
        softmax_low,
        attended,
        normed_one,
        scaled_one,
        hidden,
        pre_act,
        activated,
        normed_two,
        scaled_two,
    )
    return (result, saved)


def backward_parts(inputs_block, block_segments, weights, grad_out):
    (
        input_weight,
        input_bias,
        output_weight,
        output_bias,
        first_gain,
        first_shift,
        expand_weight,
        expand_bias,
        contract_weight,
        contract_bias,
        second_gain,
        second_shift,
    ) = weights
    row_count, model_width = inputs_block.shape
    head_size = model_width // HEADS
    score_scale = head_size ** (-0.5)
    saved = forward_parts(inputs_block, block_segments, weights)[1]
    (
        queries,
        keys_part,
        values_part,
        softmax_rows,
        softmax_low,
        attended,
        normed_one,
        scaled_one,
        hidden,
        pre_act,
        activated,
        normed_two,
        scaled_two,
    ) = saved
    grad_resid_two, grad_second_gain, grad_second_shift = norm_back(
        grad_out, normed_two, scaled_two, second_gain.astype(jnp.float32)
    )
    grad_ffn = grad_resid_two.astype(jnp.bfloat16)
    grad_contract_bias = column_sums(grad_ffn)
    grad_contract_weight = weight_grad(activated, grad_ffn)
    grad_pre = (back_product(grad_ffn, contract_weight) * gelu_slope(pre_act)).astype(jnp.bfloat16)
    grad_expand_bias = column_sums(grad_pre)
    grad_expand_weight = weight_grad(hidden, grad_pre)
    grad_hidden = grad_resid_two + back_product(grad_pre, expand_weight)
    grad_resid_one, grad_first_gain, grad_first_shift = norm_back(
        grad_hidden, normed_one, scaled_one, first_gain.astype(jnp.float32)
    )
    grad_branch = grad_resid_one.astype(jnp.bfloat16)
    grad_output_bias = column_sums(grad_branch)
    grad_output_weight = weight_grad(attended, grad_branch)
    grad_attended = (
        back_product(grad_branch, output_weight)
        .astype(jnp.bfloat16)
        .reshape(row_count, HEADS, head_size)
    )
    grad_probs = jnp.einsum(
        "qhd,khd->hqk", grad_attended, values_part, preferred_element_type=jnp.float32
    )
    grad_scores = (
        softmax_rows * (grad_probs - jnp.sum(softmax_rows * grad_probs, axis=2, keepdims=True))
    ).astype(jnp.bfloat16)
    grad_queries = (
        jnp.einsum("hqk,khd->qhd", grad_scores, keys_part, preferred_element_type=jnp.float32)
        * score_scale
    )
    grad_keys = (
        jnp.einsum("hqk,qhd->khd", grad_scores, queries, preferred_element_type=jnp.float32)
        * score_scale
    )
    grad_values = jnp.einsum(
        "hqk,qhd->khd", softmax_low, grad_attended, preferred_element_type=jnp.float32
    )
    grad_projected = jnp.concatenate(
        [
            grad_queries.reshape(row_count, model_width),
            grad_keys.reshape(row_count, model_width),
            grad_values.reshape(row_count, model_width),
        ],
        axis=1,
    ).astype(jnp.bfloat16)
    projected_sums = column_sums(grad_projected)
    grad_input_bias = jnp.concatenate(
        [projected_sums[:model_width], projected_sums[2 * model_width :]]
    )
    grad_input_weight = weight_grad(inputs_block, grad_projected)
    grad_inputs = grad_resid_one + back_product(grad_projected, input_weight)
    grads = (
        grad_input_weight,
        grad_input_bias,
        grad_output_weight,
        grad_output_bias,
        grad_first_gain,
        grad_first_shift,
        grad_expand_weight,
        grad_expand_bias,
        grad_contract_weight,
        grad_contract_bias,
        grad_second_gain,
        grad_second_shift,
    )
    return (grad_inputs, grads)


def on_device(
    tokens,
    segment_ids,
    depth,
    input_weight,
    input_bias,
    output_weight,
    output_bias,
    first_gain,
    first_shift,
    expand_weight,
    expand_bias,
    contract_weight,
    contract_bias,
    second_gain,
    second_shift,
    cotangent,
):
    masters = (
        input_weight,
        input_bias,
        output_weight,
        output_bias,
        first_gain,
        first_shift,
        expand_weight,
        expand_bias,
        contract_weight,
        contract_bias,
        second_gain,
        second_shift,
    )
    low_masters = [master[0].astype(jnp.bfloat16) for master in masters]
    gathered = (
        lax.all_gather(low_masters[0], "dp", axis=0, tiled=True),
        lax.all_gather(low_masters[1], "dp", axis=0, tiled=True),
        lax.all_gather(low_masters[2], "dp", axis=0, tiled=True),
        lax.all_gather(low_masters[3], "dp", axis=0, tiled=True),
        lax.all_gather(low_masters[4], "dp", axis=0, tiled=True),
        lax.all_gather(low_masters[5], "dp", axis=0, tiled=True),
        lax.all_gather(low_masters[6], "dp", axis=0, tiled=True),
        lax.all_gather(low_masters[7], "dp", axis=0, tiled=True),
        lax.all_gather(low_masters[8], "dp", axis=0, tiled=True),
        lax.all_gather(low_masters[9], "dp", axis=0, tiled=True),
        lax.all_gather(low_masters[10], "dp", axis=0, tiled=True),
        lax.all_gather(low_masters[11], "dp", axis=0, tiled=True),
    )
    section_index = lax.axis_index("section")
    first_section = section_index == 0
    keep_layer = jnp.logical_or(first_section, depth[0] > 9)
    token_blocks = tokens.reshape(MICRO, -1, D)
    seg_blocks = segment_ids.reshape(MICRO, -1)
    grad_blocks = cotangent.reshape(MICRO, -1, D)
    row_count = token_blocks.shape[1]

    def run_forward(operand):
        return forward_parts(operand[0], operand[1], gathered)[0].astype(jnp.bfloat16)

    def skip_forward(operand):
        return operand[0]

    sent = jnp.zeros((row_count, D), jnp.bfloat16)
    inputs_list = []
    outputs_list = []
    for tick_index in range(MICRO + 1):
        arrived = shifted(sent, "section", 1)
        own_block = token_blocks[min(tick_index, MICRO - 1)]
        current = jnp.where(first_section, own_block, arrived)
        micro_index = tick_index - section_index
        clipped = jnp.clip(micro_index, 0, MICRO - 1)
        block_segments = lax.dynamic_index_in_dim(seg_blocks, clipped, 0, keepdims=False)
        working = jnp.logical_and(
            keep_layer, jnp.logical_and(micro_index >= 0, micro_index < MICRO)
        )
        result = lax.cond(working, run_forward, skip_forward, (current, block_segments))
        inputs_list.append(current)
        outputs_list.append(result)
        sent = result
    kept_inputs = lax.dynamic_slice_in_dim(jnp.stack(inputs_list), section_index, MICRO, 0)
    layer_out = lax.dynamic_slice_in_dim(jnp.stack(outputs_list), section_index, MICRO, 0).reshape(
        1, -1, D
    )
    weights_back = (
        lax.all_gather(low_masters[0], "dp", axis=0, tiled=True),
        lax.all_gather(low_masters[1], "dp", axis=0, tiled=True),
        lax.all_gather(low_masters[2], "dp", axis=0, tiled=True),
        lax.all_gather(low_masters[3], "dp", axis=0, tiled=True),
        lax.all_gather(low_masters[4], "dp", axis=0, tiled=True),
        lax.all_gather(low_masters[5], "dp", axis=0, tiled=True),
        lax.all_gather(low_masters[6], "dp", axis=0, tiled=True),
        lax.all_gather(low_masters[7], "dp", axis=0, tiled=True),
        lax.all_gather(low_masters[8], "dp", axis=0, tiled=True),
        lax.all_gather(low_masters[9], "dp", axis=0, tiled=True),
        lax.all_gather(low_masters[10], "dp", axis=0, tiled=True),
        lax.all_gather(low_masters[11], "dp", axis=0, tiled=True),
    )

    def run_backward(operand):
        return backward_parts(operand[0], operand[1], weights_back, operand[2].astype(jnp.float32))

    def skip_backward(operand):
        return (
            operand[2].astype(jnp.float32),
            tuple((jnp.zeros(weight.shape, jnp.float32) for weight in weights_back)),
        )

    totals = tuple((jnp.zeros(weight.shape, jnp.float32) for weight in weights_back))
    sent_back = jnp.zeros((row_count, D), jnp.bfloat16)
    grads_list = []
    for tick_index in range(MICRO + 1):
        arrived = shifted(sent_back, "section", -1)
        own_grad = grad_blocks[min(tick_index, MICRO - 1)]
        incoming = jnp.where(first_section, arrived, own_grad)
        micro_index = tick_index - 1 + section_index
        clipped = jnp.clip(micro_index, 0, MICRO - 1)
        block_in = lax.dynamic_index_in_dim(kept_inputs, clipped, 0, keepdims=False)
        block_segments = lax.dynamic_index_in_dim(seg_blocks, clipped, 0, keepdims=False)
        working = jnp.logical_and(
            keep_layer, jnp.logical_and(micro_index >= 0, micro_index < MICRO)
        )
        grad_in, grads = lax.cond(
            working, run_backward, skip_backward, (block_in, block_segments, incoming)
        )
        sent_back = grad_in.astype(jnp.bfloat16)
        grads_list.append(sent_back)
        totals = tuple((total_part + new_part for total_part, new_part in zip(totals, grads)))
    shards = (
        lax.psum_scatter(totals[0], "dp", scatter_dimension=0, tiled=True),
        lax.psum_scatter(totals[1], "dp", scatter_dimension=0, tiled=True),
        lax.psum_scatter(totals[2], "dp", scatter_dimension=0, tiled=True),
        lax.psum_scatter(totals[3], "dp", scatter_dimension=0, tiled=True),
        lax.psum_scatter(totals[4], "dp", scatter_dimension=0, tiled=True),
        lax.psum_scatter(totals[5], "dp", scatter_dimension=0, tiled=True),
        lax.psum_scatter(totals[6], "dp", scatter_dimension=0, tiled=True),
        lax.psum_scatter(totals[7], "dp", scatter_dimension=0, tiled=True),
        lax.psum_scatter(totals[8], "dp", scatter_dimension=0, tiled=True),
        lax.psum_scatter(totals[9], "dp", scatter_dimension=0, tiled=True),
        lax.psum_scatter(totals[10], "dp", scatter_dimension=0, tiled=True),
        lax.psum_scatter(totals[11], "dp", scatter_dimension=0, tiled=True),
    )
    grads_out = lax.dynamic_slice_in_dim(
        jnp.stack(grads_list), 1 - section_index, MICRO, 0
    ).reshape(1, -1, D)
    return (
        layer_out,
        grads_out,
        shards[0][None],
        shards[1][None],
        shards[2][None],
        shards[3][None],
        shards[4][None],
        shards[5][None],
        shards[6][None],
        shards[7][None],
        shards[8][None],
        shards[9][None],
        shards[10][None],
        shards[11][None],
    )


def solution(mesh):
    in_specs = (
        P("dp", None),
        P("dp"),
        P("dp"),
        P("section", "dp", None),
        P("section", "dp"),
        P("section", "dp", None),
        P("section", "dp"),
        P("section", "dp"),
        P("section", "dp"),
        P("section", "dp", None),
        P("section", "dp"),
        P("section", "dp", None),
        P("section", "dp"),
        P("section", "dp"),
        P("section", "dp"),
        P("dp", None),
    )
    out_specs = (
        P("section", "dp", None),
        P("section", "dp", None),
        P("section", "dp", None),
        P("section", "dp"),
        P("section", "dp", None),
        P("section", "dp"),
        P("section", "dp"),
        P("section", "dp"),
        P("section", "dp", None),
        P("section", "dp"),
        P("section", "dp", None),
        P("section", "dp"),
        P("section", "dp"),
        P("section", "dp"),
    )
    return jax.shard_map(
        on_device, mesh=mesh, in_specs=in_specs, out_specs=out_specs, check_vma=False
    )
```

profile of v0, /device:TPU:1, one launch (start us, length us, event | category | flops | bytes accessed | tf_op | source)
XLA Modules:
  0.0 1540.4 jit_solution(5055521955754888712)
XLA Ops:
  13.8 4.1 collective-permute-start
  29.3 325.1 %all-reduce.23 = (bf16[1536]{0:T(1024)(128)(2,1)S(1)}, bf16[768]{0:T(1024)(128)(2,1)S(1)}, bf16[768]{0:T(1024)(128)(2,1)}, bf16[768]{0:T(1024)(128)(2,1)}, bf16[...) all-reduce(bf16[1536]{0:T(1024)(128)(2,1)S(1)} %dynamic-update-slic, ...), channel_id=3, replica_groups=mesh['section'=2,'dp'=64] {'dp'}, use_global_device_ids=true, to_apply=%add | all-reduce | flops 9216 | bytes 36864 | tf_op jit(solution)/shard_map/all_gather | solution.py:273
  357.4 5.3 copy.220
  362.7 7.7 copy.219
  370.5 26.3 %conditional.6 = (bf16[256,768]{1,0:T(8,128)(2,1)}) conditional(s32[]{:T(128)} %convert_element_type.738, bf16[256,768]{1,0:T(8,128)(2,1)S(1)} %slice_select_fusion.1, (bf16[256,768]{1,0:T(8,128)(2,1)S(1)}, bf16[768,2304]{1,0:T(8,128)(2,1)}, bf16[1536]{0:T(1024)(128)(2,1)S(1)}, s32[]{:T(128)}, s32[2,256]{1,0:T(2,128)S(1)}, ...), branch_computations={%region_0.1_spmd, %region_1.8_spmd} | conditional | flops 3888994048 | bytes 34593000 | solution.py:312
  382.4 13.0 fusion.379
  404.2 29.4 %conditional.7 = (bf16[256,768]{1,0:T(8,128)(2,1)S(1)}) conditional(s32[]{:T(128)} %convert_element_type.763, bf16[256,768]{1,0:T(8,128)(2,1)S(1)} %broadcast_select_fusion.3, (bf16[256,768]{1,0:T(8,128)(2,1)S(1)}, bf16[768,2304]{1,0:T(8,128)(2,1)}, bf16[1536]{0:T(1024)(128)(2,1)S(1)}, s32[]{:T(128)}, s32[2,256]{1,0:T(2,128)}, ...), branch_computations={%region_8.9_spmd, %region_9.16_spmd} | conditional | flops 3888994048 | bytes 37738760 | solution.py:312
  419.3 13.3 fusion.384
  440.7 25.8 %conditional.9 = (f32[768,2304]{1,0:T(8,128)}, f32[1536]{0:T(1024)S(1)}, f32[768,768]{1,0:T(8,128)}, f32[768]{0:T(1024)S(1)}, f32[768]{0:T(1024)S(1)}, /*index=5...) conditional(s32[]{:T(128)} %convert_element_type.765, ...), branch_computations={%region_24.25_spmd, %region_25.45_spmd} | conditional | flops 11577534464 | bytes 240108320 | solution.py:358
  446.3 4.7 broadcast.1422
  451.6 4.1 broadcast.1424
  467.9 7.4 collective-permute-done.4
  476.4 65.9 %conditional.10 = (f32[768,2304]{1,0:T(8,128)}, f32[1536]{0:T(1024)S(1)}, f32[768,768]{1,0:T(8,128)}, f32[768]{0:T(1024)S(1)}, f32[768]{0:T(1024)S(1)}, /*index=...) conditional(s32[]{:T(128)} %convert_element_type.766, ...), branch_computations={%region_45.46_spmd, %region_46.66_spmd} | conditional | flops 11577534464 | bytes 243254112 | solution.py:358
  486.0 4.3 fusion.399
  493.7 10.1 fusion.268
  523.6 4.1 fusion.298
  530.7 5.2 fusion.410
  535.9 5.1 fusion.310
  552.1 63.2 %conditional.11 = (f32[768,2304]{1,0:T(8,128)}, f32[1536]{0:T(1024)}, f32[768,768]{1,0:T(8,128)}, f32[768]{0:T(1024)}, f32[768]{0:T(1024)}, /*index=5*/f32[768]{...) conditional(s32[]{:T(128)} %convert_element_type.767, ...), branch_computations={%region_66.67_spmd, %region_67.87_spmd} | conditional | flops 11577534464 | bytes 238461536 | solution.py:358
  562.1 4.3 fusion.405
  569.8 10.1 fusion.320
  597.0 4.0 fusion.350
  603.9 5.1 fusion.411
  609.0 5.0 fusion.362
  615.4 14.1 add_add_fusion
  629.5 11.1 add_add_fusion.2
  640.7 14.8 add_add_fusion.1
  659.0 264.6 %fusion.371 = (f32[16,2304]{1,0:T(8,128)S(1)}, f32[16,768]{1,0:T(8,128)S(1)}, f32[16,3072]{1,0:T(8,128)S(1)}) fusion(f32[768,2304]{1,0:T(8,128)} %add_add_fusion.2, f32[768,768]{1,0:T(8,128)S(1)} %add_add_fusion.3, f32[768,3072]{1,0:T(8,128)} %add_add_fusion.1), kind=kCustom, calls=%all-reduce-scatter.3 | all-reduce-scatter fusion | flops 6291457 | bytes 19268096
  925.0 8.1 collective-permute-start.35
  935.7 14.0 collective-permute-start.37
  952.5 9.2 collective-permute-start.31
  965.5 6.5 collective-permute-start.28
  993.9 316.1 %all-reduce.22 = (f32[1536]{0:T(1024)S(1)}, f32[768]{0:T(1024)S(1)}, f32[768]{0:T(1024)S(1)}, f32[768]{0:T(1024)S(1)}, f32[3072]{0:T(1024)}, /*index=5*/f32[768]{0:T(1024)S(1)}, f32[768]{0:T(1024)}, f32[768]{0:T(1024)}) all-reduce(f32[1536]{0:T(1024)S(1)} %add_add_fusion.5, ...), channel_id=15, replica_groups=mesh['section'=2,'dp'=64] {'dp'}, use_global_device_ids=true, to_apply=%region_88.89.clone | all-reduce | flops 9216 | bytes 73728
  1315.3 11.4 collective-permute-start.15
  1327.9 7.7 collective-permute-start.14
  1337.3 4.4 collective-permute-start.12
  1341.7 4.0 collective-permute-start.11
  1352.2 4.5 collective-permute-start.8
  1356.7 5.8 collective-permute-start.7
  1364.5 4.4 collective-permute-start.53
  1371.5 4.5 collective-permute-start.52
  1376.1 4.0 collective-permute-start.51
  1389.4 21.7 %collective-permute-start.46 = (f32[16,3072]{1,0:T(8,128)S(1)}, f32[16,3072]{1,0:T(8,128)S(1)}, u32[]{:S(2)}, u32[]{:S(2)}) collective-permute-start(f32[16,3072]{1,0:T(8,128)S(1)} %get-tuple-element.922), channel_id=1, source_target_pairs={{0,9},{1,10},{2,11},{3,12},{4,13},{5,14},{6,15},{7,16},{8,17},{9,1... | collective-permute-start | bytes 589832
  1413.1 8.9 collective-permute-start.44
  1424.6 14.0 concatenate.97
  1439.4 28.9 %concatenate.96 = f32[268,2304]{1,0:T(8,128)} concatenate(f32[12,2304]{1,0:T(8,128)} %copy-done.64, f32[16,2304]{1,0:T(8,128)S(1)} %collective-permute-done.20, f32[16,2304]{1,0:T(8,128)} %copy-done.65, f32[16,2304]{1,0:T(8,128)} %copy-done.66, f32[16,2304]{1,0:T(8,128)} %copy-done.67, f32[16,2304]{1,0:T(8,128)} %copy-done.68, f32[16,2304]{1,0:T(8,128)} %copy-done.69, ...), dimensions={0} | concatenate | bytes 4939776
  1468.2 4.6 collective-permute-start.42
  1490.6 41.2 %concatenate.98 = f32[268,3072]{1,0:T(8,128)} concatenate(f32[12,3072]{1,0:T(8,128)S(1)} %collective-permute-done.53, f32[16,3072]{1,0:T(8,128)S(1)} %collective-permute-done.52, f32[16,3072]{1,0:T(8,128)S(1)} %collective-permute-done.51, f32[16,3072]{1,0:T(8,128)S(1)} %collective-permute-done.50, f32[16,3072]{1,0:T(8,128)S(1)} %collective-permute-done.49, ...), dimensions={0} | concatenate | bytes 6586368
  (594 shorter events, 234.8 us)
Async XLA Ops:
  7.2 348.4 %all-gather.19.cloned.1.call-start = ((), (), s32[]{:S(2)}) async-start(), calls=%async_computation.3 | async-start | bytes 2396160 | tf_op jit(solution)/shard_map/all_gather | solution.py:274
  8.7 348.8 %all-gather.17.cloned.1.call-start = ((), (), s32[]{:S(2)}) async-start(), calls=%async_computation.2 | async-start | bytes 7188480 | tf_op jit(solution)/shard_map/all_gather | solution.py:272
  10.4 352.4 %all-gather.21.cloned.1.call-start = ((), (), s32[]{:S(2)}) async-start(), calls=%async_computation.4 | async-start | bytes 9584640 | tf_op jit(solution)/shard_map/all_gather | solution.py:278
  12.1 358.3 %all-gather.23.cloned.1.call-start = ((), (), s32[]{:S(2)}) async-start(), calls=%async_computation.5 | async-start | bytes 4792320 | tf_op jit(solution)/shard_map/all_gather | solution.py:280
  13.7 1519.9 %reduce-scatter.8.cloned.1.call-start = ((), (), s32[]{:S(2)}) async-start(), calls=%async_computation.1 | async-start | bytes 9584640 | tf_op jit(solution)/shard_map/reduce_scatter | solution.py:373
  13.8 340.6 %collective-permute-start = (bf16[256,768]{1,0:T(8,128)(2,1)S(1)}, bf16[256,768]{1,0:T(8,128)(2,1)S(1)}, u32[]{:S(2)}, u32[]{:S(2)}) collective-permute-start(bf16[256,768]{1,0:T(8,128)(2,1)S(1)} %broadcast.1548), channel_id=1, source_target_pairs={{0,64},{1,65},{2,66},{3,67},{4,68},{5,69},{6,70},{7,71},{8,72},{9,... | collective-permute-start | bytes 1179656 | tf_op jit(solution)/shard_map/ppermute | solution.py:17
  398.1 36.8 %collective-permute-start.3 = (bf16[256,768]{1,0:T(8,128)(2,1)}, bf16[256,768]{1,0:T(8,128)(2,1)}, u32[]{:S(2)}, u32[]{:S(2)}) collective-permute-start(bf16[256,768]{1,0:T(8,128)(2,1)} %copy-done.58), channel_id=1, source_target_pairs={{64,0},{65,1},{66,2},{67,3},{68,4},{69,5},{70,6},{71,7},{72,8},{73... | collective-permute-start | bytes 1179656 | tf_op jit(solution)/shard_map/ppermute | solution.py:17
  923.7 28.9 %collective-permute-start.36 = (f32[16,768]{1,0:T(8,128)S(1)}, f32[16,768]{1,0:T(8,128)S(1)}, u32[]{:S(2)}, u32[]{:S(2)}) collective-permute-start(f32[16,768]{1,0:T(8,128)S(1)} %get-tuple-element.921), channel_id=1, source_target_pairs={{0,15},{1,16},{2,17},{3,18},{4,19},{5,20},{6,21},{7,22},{8,23},{9,... | collective-permute-start | bytes 147464
  925.0 36.8 %collective-permute-start.35 = (f32[16,768]{1,0:T(8,128)S(1)}, f32[16,768]{1,0:T(8,128)S(1)}, u32[]{:S(2)}, u32[]{:S(2)}) collective-permute-start(f32[16,768]{1,0:T(8,128)S(1)} %get-tuple-element.921), channel_id=1, source_target_pairs={{0,14},{1,15},{2,16},{3,17},{4,18},{5,19},{6,20},{7,21},{8,22},{9,... | collective-permute-start | bytes 147464
  933.1 30.8 %collective-permute-start.34 = (f32[16,768]{1,0:T(8,128)S(1)}, f32[16,768]{1,0:T(8,128)S(1)}, u32[]{:S(2)}, u32[]{:S(2)}) collective-permute-start(f32[16,768]{1,0:T(8,128)S(1)} %get-tuple-element.921), channel_id=1, source_target_pairs={{0,13},{1,14},{2,15},{3,16},{4,17},{5,18},{6,19},{7,20},{8,21},{9,... | collective-permute-start | bytes 147464
  934.4 31.1 %collective-permute-start.33 = (f32[16,768]{1,0:T(8,128)S(1)}, f32[16,768]{1,0:T(8,128)S(1)}, u32[]{:S(2)}, u32[]{:S(2)}) collective-permute-start(f32[16,768]{1,0:T(8,128)S(1)} %get-tuple-element.921), channel_id=1, source_target_pairs={{0,12},{1,13},{2,14},{3,15},{4,16},{5,17},{6,18},{7,19},{8,20},{9,... | collective-permute-start | bytes 147464
  935.7 15.5 %collective-permute-start.37 = (f32[12,768]{1,0:T(8,128)S(1)}, f32[12,768]{1,0:T(8,128)S(1)}, u32[]{:S(2)}, u32[]{:S(2)}) collective-permute-start(f32[12,768]{1,0:T(8,128)S(1)} %slice.212), channel_id=1, source_target_pairs={{0,16},{1,17},{2,18},{3,19},{4,20},{5,21},{6,22},{7,23},{8,24},{9,... | collective-permute-start | bytes 110600
  951.2 20.8 %collective-permute-start.32 = (f32[16,768]{1,0:T(8,128)S(1)}, f32[16,768]{1,0:T(8,128)S(1)}, u32[]{:S(2)}, u32[]{:S(2)}) collective-permute-start(f32[16,768]{1,0:T(8,128)S(1)} %get-tuple-element.921), channel_id=1, source_target_pairs={{0,11},{1,12},{2,13},{3,14},{4,15},{5,16},{6,17},{7,18},{8,19},{9,... | collective-permute-start | bytes 147464
  952.5 23.0 %collective-permute-start.31 = (f32[16,768]{1,0:T(8,128)S(1)}, f32[16,768]{1,0:T(8,128)S(1)}, u32[]{:S(2)}, u32[]{:S(2)}) collective-permute-start(f32[16,768]{1,0:T(8,128)S(1)} %get-tuple-element.921), channel_id=1, source_target_pairs={{0,10},{1,11},{2,12},{3,13},{4,14},{5,15},{6,16},{7,17},{8,18},{9,... | collective-permute-start | bytes 147464
  961.8 15.3 collective-permute-start.30
  963.9 17.4 %collective-permute-start.29 = (f32[16,768]{1,0:T(8,128)S(1)}, f32[16,768]{1,0:T(8,128)S(1)}, u32[]{:S(2)}, u32[]{:S(2)}) collective-permute-start(f32[16,768]{1,0:T(8,128)S(1)} %get-tuple-element.921), channel_id=1, source_target_pairs={{0,8},{1,9},{2,10},{3,11},{4,12},{5,13},{6,14},{7,15},{8,16},{9,17... | collective-permute-start | bytes 147464
  965.5 18.1 %collective-permute-start.28 = (f32[16,768]{1,0:T(8,128)S(1)}, f32[16,768]{1,0:T(8,128)S(1)}, u32[]{:S(2)}, u32[]{:S(2)}) collective-permute-start(f32[16,768]{1,0:T(8,128)S(1)} %get-tuple-element.921), channel_id=1, source_target_pairs={{0,7},{1,8},{2,9},{3,10},{4,11},{5,12},{6,13},{7,14},{8,15},{9,16}... | collective-permute-start | bytes 147464
  972.1 15.2 collective-permute-start.27
  981.3 333.9 %collective-permute-start.20 = (f32[16,2304]{1,0:T(8,128)S(1)}, f32[16,2304]{1,0:T(8,128)S(1)}, u32[]{:S(2)}, u32[]{:S(2)}) collective-permute-start(f32[16,2304]{1,0:T(8,128)S(1)} %get-tuple-element.920), channel_id=1, source_target_pairs={{0,15},{1,16},{2,17},{3,18},{4,19},{5,20},{6,21},{7,22},{8,23},{9,... | collective-permute-start | bytes 442376
  983.6 326.4 %collective-permute-start.24 = (f32[16,768]{1,0:T(8,128)S(1)}, f32[16,768]{1,0:T(8,128)}, u32[]{:S(2)}, u32[]{:S(2)}) collective-permute-start(f32[16,768]{1,0:T(8,128)S(1)} %get-tuple-element.921), channel_id=1, source_target_pairs={{0,3},{1,4},{2,5},{3,6},{4,7},{5,8},{6,9},{7,10},{8,11},{9,12},{10... | collective-permute-start | bytes 147464
  987.3 324.0 %collective-permute-start.23 = (f32[16,768]{1,0:T(8,128)S(1)}, f32[16,768]{1,0:T(8,128)}, u32[]{:S(2)}, u32[]{:S(2)}) collective-permute-start(f32[16,768]{1,0:T(8,128)S(1)} %get-tuple-element.921), channel_id=1, source_target_pairs={{0,2},{1,3},{2,4},{3,5},{4,6},{5,7},{6,8},{7,9},{8,10},{9,11},{10,... | collective-permute-start | bytes 147464
  989.9 322.7 %collective-permute-start.22 = (f32[16,768]{1,0:T(8,128)S(1)}, f32[16,768]{1,0:T(8,128)}, u32[]{:S(2)}, u32[]{:S(2)}) collective-permute-start(f32[16,768]{1,0:T(8,128)S(1)} %get-tuple-element.921), channel_id=1, source_target_pairs={{0,1},{1,2},{2,3},{3,4},{4,5},{5,6},{6,7},{7,8},{8,9},{9,10},{10,1... | collective-permute-start | bytes 147464
  991.8 322.1 %collective-permute-start.21 = (f32[12,2304]{1,0:T(8,128)S(1)}, f32[12,2304]{1,0:T(8,128)S(1)}, u32[]{:S(2)}, u32[]{:S(2)}) collective-permute-start(f32[12,2304]{1,0:T(8,128)S(1)} %slice.211), channel_id=1, source_target_pairs={{0,16},{1,17},{2,18},{3,19},{4,20},{5,21},{6,22},{7,23},{8,24},{9,... | collective-permute-start | bytes 331784
  1310.0 17.9 %collective-permute-start.19 = (f32[16,2304]{1,0:T(8,128)S(1)}, f32[16,2304]{1,0:T(8,128)S(1)}, u32[]{:S(2)}, u32[]{:S(2)}) collective-permute-start(f32[16,2304]{1,0:T(8,128)S(1)} %get-tuple-element.920), channel_id=1, source_target_pairs={{0,14},{1,15},{2,16},{3,17},{4,18},{5,19},{6,20},{7,21},{8,22},{9,... | collective-permute-start | bytes 442376
  1311.3 24.4 %collective-permute-start.18 = (f32[16,2304]{1,0:T(8,128)S(1)}, f32[16,2304]{1,0:T(8,128)S(1)}, u32[]{:S(2)}, u32[]{:S(2)}) collective-permute-start(f32[16,2304]{1,0:T(8,128)S(1)} %get-tuple-element.920), channel_id=1, source_target_pairs={{0,13},{1,14},{2,15},{3,16},{4,17},{5,18},{6,19},{7,20},{8,21},{9,... | collective-permute-start | bytes 442376
  1312.6 24.7 %collective-permute-start.17 = (f32[16,2304]{1,0:T(8,128)S(1)}, f32[16,2304]{1,0:T(8,128)S(1)}, u32[]{:S(2)}, u32[]{:S(2)}) collective-permute-start(f32[16,2304]{1,0:T(8,128)S(1)} %get-tuple-element.920), channel_id=1, source_target_pairs={{0,12},{1,13},{2,14},{3,15},{4,16},{5,17},{6,18},{7,19},{8,20},{9,... | collective-permute-start | bytes 442376
  1313.9 27.8 %collective-permute-start.16 = (f32[16,2304]{1,0:T(8,128)S(1)}, f32[16,2304]{1,0:T(8,128)S(1)}, u32[]{:S(2)}, u32[]{:S(2)}) collective-permute-start(f32[16,2304]{1,0:T(8,128)S(1)} %get-tuple-element.920), channel_id=1, source_target_pairs={{0,11},{1,12},{2,13},{3,14},{4,15},{5,16},{6,17},{7,18},{8,19},{9,... | collective-permute-start | bytes 442376
  1315.3 30.5 %collective-permute-start.15 = (f32[16,2304]{1,0:T(8,128)S(1)}, f32[16,2304]{1,0:T(8,128)S(1)}, u32[]{:S(2)}, u32[]{:S(2)}) collective-permute-start(f32[16,2304]{1,0:T(8,128)S(1)} %get-tuple-element.920), channel_id=1, source_target_pairs={{0,10},{1,11},{2,12},{3,13},{4,14},{5,15},{6,16},{7,17},{8,18},{9,... | collective-permute-start | bytes 442376
  1327.9 21.3 %collective-permute-start.14 = (f32[16,2304]{1,0:T(8,128)S(1)}, f32[16,2304]{1,0:T(8,128)S(1)}, u32[]{:S(2)}, u32[]{:S(2)}) collective-permute-start(f32[16,2304]{1,0:T(8,128)S(1)} %get-tuple-element.920), channel_id=1, source_target_pairs={{0,9},{1,10},{2,11},{3,12},{4,13},{5,14},{6,15},{7,16},{8,17},{9,1... | collective-permute-start | bytes 442376
  1335.7 16.5 %collective-permute-start.13 = (f32[16,2304]{1,0:T(8,128)S(1)}, f32[16,2304]{1,0:T(8,128)S(1)}, u32[]{:S(2)}, u32[]{:S(2)}) collective-permute-start(f32[16,2304]{1,0:T(8,128)S(1)} %get-tuple-element.920), channel_id=1, source_target_pairs={{0,8},{1,9},{2,10},{3,11},{4,12},{5,13},{6,14},{7,15},{8,16},{9,17... | collective-permute-start | bytes 442376
  1337.3 19.4 %collective-permute-start.12 = (f32[16,2304]{1,0:T(8,128)S(1)}, f32[16,2304]{1,0:T(8,128)S(1)}, u32[]{:S(2)}, u32[]{:S(2)}) collective-permute-start(f32[16,2304]{1,0:T(8,128)S(1)} %get-tuple-element.920), channel_id=1, source_target_pairs={{0,7},{1,8},{2,9},{3,10},{4,11},{5,12},{6,13},{7,14},{8,15},{9,16}... | collective-permute-start | bytes 442376
  1341.7 20.8 %collective-permute-start.11 = (f32[16,2304]{1,0:T(8,128)S(1)}, f32[16,2304]{1,0:T(8,128)S(1)}, u32[]{:S(2)}, u32[]{:S(2)}) collective-permute-start(f32[16,2304]{1,0:T(8,128)S(1)} %get-tuple-element.920), channel_id=1, source_target_pairs={{0,6},{1,7},{2,8},{3,9},{4,10},{5,11},{6,12},{7,13},{8,14},{9,15},... | collective-permute-start | bytes 442376
  1345.8 18.7 %collective-permute-start.10 = (f32[16,2304]{1,0:T(8,128)S(1)}, f32[16,2304]{1,0:T(8,128)S(1)}, u32[]{:S(2)}, u32[]{:S(2)}) collective-permute-start(f32[16,2304]{1,0:T(8,128)S(1)} %get-tuple-element.920), channel_id=1, source_target_pairs={{0,5},{1,6},{2,7},{3,8},{4,9},{5,10},{6,11},{7,12},{8,13},{9,14},{... | collective-permute-start | bytes 442376
  1349.2 22.3 %collective-permute-start.9 = (f32[16,2304]{1,0:T(8,128)S(1)}, f32[16,2304]{1,0:T(8,128)S(1)}, u32[]{:S(2)}, u32[]{:S(2)}) collective-permute-start(f32[16,2304]{1,0:T(8,128)S(1)} %get-tuple-element.920), channel_id=1, source_target_pairs={{0,4},{1,5},{2,6},{3,7},{4,8},{5,9},{6,10},{7,11},{8,12},{9,13},{1... | collective-permute-start | bytes 442376
  1352.2 23.8 %collective-permute-start.8 = (f32[16,2304]{1,0:T(8,128)S(1)}, f32[16,2304]{1,0:T(8,128)S(1)}, u32[]{:S(2)}, u32[]{:S(2)}) collective-permute-start(f32[16,2304]{1,0:T(8,128)S(1)} %get-tuple-element.920), channel_id=1, source_target_pairs={{0,3},{1,4},{2,5},{3,6},{4,7},{5,8},{6,9},{7,10},{8,11},{9,12},{10... | collective-permute-start | bytes 442376
  1356.7 23.4 %collective-permute-start.7 = (f32[16,2304]{1,0:T(8,128)S(1)}, f32[16,2304]{1,0:T(8,128)S(1)}, u32[]{:S(2)}, u32[]{:S(2)}) collective-permute-start(f32[16,2304]{1,0:T(8,128)S(1)} %get-tuple-element.920), channel_id=1, source_target_pairs={{0,2},{1,3},{2,4},{3,5},{4,6},{5,7},{6,8},{7,9},{8,10},{9,11},{10,... | collective-permute-start | bytes 442376
  1362.6 20.8 %collective-permute-start.6 = (f32[16,2304]{1,0:T(8,128)S(1)}, f32[16,2304]{1,0:T(8,128)S(1)}, u32[]{:S(2)}, u32[]{:S(2)}) collective-permute-start(f32[16,2304]{1,0:T(8,128)S(1)} %get-tuple-element.920), channel_id=1, source_target_pairs={{0,1},{1,2},{2,3},{3,4},{4,5},{5,6},{6,7},{7,8},{8,9},{9,10},{10,1... | collective-permute-start | bytes 442376
  1364.5 20.2 %collective-permute-start.53 = (f32[12,3072]{1,0:T(8,128)S(1)}, f32[12,3072]{1,0:T(8,128)S(1)}, u32[]{:S(2)}, u32[]{:S(2)}) collective-permute-start(f32[12,3072]{1,0:T(8,128)S(1)} %slice.213), channel_id=1, source_target_pairs={{0,16},{1,17},{2,18},{3,19},{4,20},{5,21},{6,22},{7,23},{8,24},{9,... | collective-permute-start | bytes 442376
  1371.5 16.4 %collective-permute-start.52 = (f32[16,3072]{1,0:T(8,128)S(1)}, f32[16,3072]{1,0:T(8,128)S(1)}, u32[]{:S(2)}, u32[]{:S(2)}) collective-permute-start(f32[16,3072]{1,0:T(8,128)S(1)} %get-tuple-element.922), channel_id=1, source_target_pairs={{0,15},{1,16},{2,17},{3,18},{4,19},{5,20},{6,21},{7,22},{8,23},{9,... | collective-permute-start | bytes 589832
  1380.1 31.0 %collective-permute-start.50 = (f32[16,3072]{1,0:T(8,128)S(1)}, f32[16,3072]{1,0:T(8,128)S(1)}, u32[]{:S(2)}, u32[]{:S(2)}) collective-permute-start(f32[16,3072]{1,0:T(8,128)S(1)} %get-tuple-element.922), channel_id=1, source_target_pairs={{0,13},{1,14},{2,15},{3,16},{4,17},{5,18},{6,19},{7,20},{8,21},{9,... | collective-permute-start | bytes 589832
  1383.4 29.7 %collective-permute-start.49 = (f32[16,3072]{1,0:T(8,128)S(1)}, f32[16,3072]{1,0:T(8,128)S(1)}, u32[]{:S(2)}, u32[]{:S(2)}) collective-permute-start(f32[16,3072]{1,0:T(8,128)S(1)} %get-tuple-element.922), channel_id=1, source_target_pairs={{0,12},{1,13},{2,14},{3,15},{4,16},{5,17},{6,18},{7,19},{8,20},{9,... | collective-permute-start | bytes 589832
  1384.7 37.3 %collective-permute-start.48 = (f32[16,3072]{1,0:T(8,128)S(1)}, f32[16,3072]{1,0:T(8,128)S(1)}, u32[]{:S(2)}, u32[]{:S(2)}) collective-permute-start(f32[16,3072]{1,0:T(8,128)S(1)} %get-tuple-element.922), channel_id=1, source_target_pairs={{0,11},{1,12},{2,13},{3,14},{4,15},{5,16},{6,17},{7,18},{8,19},{9,... | collective-permute-start | bytes 589832
  1387.9 80.3 %collective-permute-start.47 = (f32[16,3072]{1,0:T(8,128)S(1)}, f32[16,3072]{1,0:T(8,128)S(1)}, u32[]{:S(2)}, u32[]{:S(2)}) collective-permute-start(f32[16,3072]{1,0:T(8,128)S(1)} %get-tuple-element.922), channel_id=1, source_target_pairs={{0,10},{1,11},{2,12},{3,13},{4,14},{5,15},{6,16},{7,17},{8,18},{9,... | collective-permute-start | bytes 589832
  1389.4 83.5 %collective-permute-start.46 = (f32[16,3072]{1,0:T(8,128)S(1)}, f32[16,3072]{1,0:T(8,128)S(1)}, u32[]{:S(2)}, u32[]{:S(2)}) collective-permute-start(f32[16,3072]{1,0:T(8,128)S(1)} %get-tuple-element.922), channel_id=1, source_target_pairs={{0,9},{1,10},{2,11},{3,12},{4,13},{5,14},{6,15},{7,16},{8,17},{9,1... | collective-permute-start | bytes 589832
  1411.2 64.2 %collective-permute-start.45 = (f32[16,3072]{1,0:T(8,128)S(1)}, f32[16,3072]{1,0:T(8,128)S(1)}, u32[]{:S(2)}, u32[]{:S(2)}) collective-permute-start(f32[16,3072]{1,0:T(8,128)S(1)} %get-tuple-element.922), channel_id=1, source_target_pairs={{0,8},{1,9},{2,10},{3,11},{4,12},{5,13},{6,14},{7,15},{8,16},{9,17... | collective-permute-start | bytes 589832
  1413.1 66.3 %collective-permute-start.44 = (f32[16,3072]{1,0:T(8,128)S(1)}, f32[16,3072]{1,0:T(8,128)S(1)}, u32[]{:S(2)}, u32[]{:S(2)}) collective-permute-start(f32[16,3072]{1,0:T(8,128)S(1)} %get-tuple-element.922), channel_id=1, source_target_pairs={{0,7},{1,8},{2,9},{3,10},{4,11},{5,12},{6,13},{7,14},{8,15},{9,16}... | collective-permute-start | bytes 589832
  1422.0 59.3 %collective-permute-start.43 = (f32[16,3072]{1,0:T(8,128)S(1)}, f32[16,3072]{1,0:T(8,128)S(1)}, u32[]{:S(2)}, u32[]{:S(2)}) collective-permute-start(f32[16,3072]{1,0:T(8,128)S(1)} %get-tuple-element.922), channel_id=1, source_target_pairs={{0,6},{1,7},{2,8},{3,9},{4,10},{5,11},{6,12},{7,13},{8,14},{9,15},... | collective-permute-start | bytes 589832
  1468.2 17.6 %collective-permute-start.42 = (f32[16,3072]{1,0:T(8,128)S(1)}, f32[16,3072]{1,0:T(8,128)S(1)}, u32[]{:S(2)}, u32[]{:S(2)}) collective-permute-start(f32[16,3072]{1,0:T(8,128)S(1)} %get-tuple-element.922), channel_id=1, source_target_pairs={{0,5},{1,6},{2,7},{3,8},{4,9},{5,10},{6,11},{7,12},{8,13},{9,14},{... | collective-permute-start | bytes 589832
  (144 other events, 5572.9 us)
Sparse Core Ops, SparseCore 0:
  11.9 71.9 all-gather.18
  87.7 74.8 all-gather.16
  166.5 82.5 all-gather.20
  252.8 70.5 all-gather.22
  629.6 262.8 reduce-scatter.7
where the time goes:
time: 1550 us; the launch traced here: 1540 us
  blocking collectives  906 us (58%)
  starting transfers between devices  199 us (13%)
  local copies, waits for them, and re-layouts  146 us (9%)
  matrix products  144 us (9%)
  other arithmetic  90 us (6%)
  waiting for transfers between devices  20.9 us (1%)
  between operations  20.7 us (1%)
    unnamed x2, blocking collectives  581 us
    all_gather x1, blocking collectives, on_device(): lax.all_gather(low_masters[1], 'dp', axis=0, tiled=True)  325 us
    unnamed x48, starting transfers between devices  188 us
    unnamed x121, local copies, waits for them, and re-layouts  104 us
    add x9, other arithmetic, on_device(): total_part + new_part  47.2 us
    dot_general x8, matrix products, weight_grad(): jnp.einsum('rk,rn->kn', left, right, preferred_element_type=jnp.float32)  32.3 us
  transfers between devices with their start and end apart: 59, of which 6 were waited for; matrix products, arithmetic and copies ran while one was open for 30% of the time, Pallas kernels for 0%

commit v1 on v0

v1 whole, which is shorter than its diff:
```python
import jax
import jax.numpy as jnp
from jax import lax
from jax.experimental import pallas as pl
from jax.experimental.pallas import tpu as pltpu
from jax.sharding import Mesh, PartitionSpec as P

D = 768
HEADS = 12
BLOCK = 256
EPS = 1e-05
Y = ("section", "yh")
ROWS = 96
BF = jnp.bfloat16
F32 = jnp.float32


def position(axis):
    if isinstance(axis, tuple):
        return lax.axis_index("yh") * 2 + lax.axis_index("section")
    return lax.axis_index(axis)


def size_of(axis):
    return 4 if isinstance(axis, tuple) else lax.axis_size(axis)


def ahead(value, axis, steps):
    count = size_of(axis)
    at = [0, 2, 1, 3] if isinstance(axis, tuple) else range(count)
    return lax.ppermute(value, axis, [(at[i], at[(i + steps) % count]) for i in range(count)])


def from_behind(value, axis):
    return [value] + [ahead(value, axis, k) for k in (1, 2, 3)]


def by_position(pieces, here):
    rising = [pieces[0], pieces[3], pieces[2], pieces[1]]
    return lax.dynamic_slice_in_dim(jnp.stack(rising + rising), (4 - here) % 4, 4, 0)


def ahead_crossed(value, steps, first):
    pairs = []
    for y in range(4):
        for z in range(4):
            for c in range(2):
                to_y, to_z = ((y + steps) % 4, z) if c == first else (y, (z + steps) % 4)
                pairs.append(
                    (
                        (((y % 2) * 2 + y // 2) * 4 + z) * 2 + c,
                        (((to_y % 2) * 2 + to_y // 2) * 4 + to_z) * 2 + c,
                    )
                )
    return lax.ppermute(value, ("section", "yh", "z", "core"), pairs)


def swap_core(value):
    return ahead(value, "core", 1)


def behind(axis, k):
    return lax.rem(position(axis) + (4 - k), 4)


class Chunks:
    def __init__(self, to, sems):
        self.to, self.sems, self.here = to, sems, set()

    def bring(self, source, block, z):
        block = block * 4 + z
        rows = pl.ds(pl.multiple_of(block * ROWS, ROWS), ROWS)
        for j in range(4):
            pltpu.make_async_copy(
                source.at[pl.ds(j * ROWS, ROWS), :], self.to.at[j, rows, :], self.sems.at[j, block]
            ).start()

    def get(self, j):
        for block in range(0 if j in self.here else 8):
            here = self.to.at[j, pl.ds(block * ROWS, ROWS), :]
            pltpu.make_async_copy(here, here, self.sems.at[j, block]).wait()
        self.here.add(j)
        return self.to[j]


def attention_chunks(layer, pieces, to, sems, vraw=None, sem_v=None):
    chunks = Chunks(to, sems)
    core = lax.axis_index("core")
    for r in range(2):

        @pl.when(core == r)
        def _():
            for k in range(4):
                z = behind("z", k)
                for yh in range(2):
                    piece = pieces[r * 8 + layer * 4 + k].at[yh]
                    if vraw is not None:
                        pltpu.make_async_copy(
                            piece.at[pl.ds(4 * ROWS, 16), :], vraw.at[yh, z], sem_v.at[yh, z]
                        ).start()
                    chunks.bring(piece, yh, z)

    return chunks


def expand_chunks(layer, pieces, to, sems):
    chunks = Chunks(to, sems)
    core = lax.axis_index("core")
    for k in range(4):
        ys = behind(Y, k)
        for r in range(2):

            @pl.when(jnp.logical_and(lax.rem(ys, 2) == layer, core == 1 - r))
            def _():
                for h in range(2):
                    for zh in range(2):
                        chunks.bring(pieces[r * 8 + h * 4 + k].at[zh], ys // 2, 2 * zh + h)

    return chunks


class Contract:
    def __init__(self, layer, pieces, to, sems):
        self.to, self.sems, self.here = to, sems, set()
        core = lax.axis_index("core")
        for j in range(4):
            yh, z = j // 2, pl.ds((j % 2) * 2, 2)
            for r in range(2):
                for x in range(4):
                    pltpu.make_async_copy(
                        pieces[r].at[x, z, yh * 2 + layer],
                        to.at[yh, z, x, core if r == 0 else 1 - core],
                        sems.at[j, core if r == 0 else 1 - core, x],
                    ).start()

    def get(self, j):
        yh, first = j // 2, (j % 2) * 2
        for r in range(0 if j in self.here else 2):
            for x in range(4):
                here = self.to.at[yh, pl.ds(first, 2), x, r]
                pltpu.make_async_copy(here, here, self.sems.at[j, r, x]).wait()
        self.here.add(j)
        return self.to[yh, first : first + 2].reshape(D, D)


class Out:
    def __init__(self, sems):
        self.sems, self.copies = sems, []

    def put(self, source, to):
        copy = pltpu.make_async_copy(source, to, self.sems.at[len(self.copies)])
        copy.start()
        self.copies.append(copy)

    def drain(self):
        for copy in self.copies:
            copy.wait()


WA = pltpu.VMEM((4, D, D), BF)
WC = pltpu.VMEM((2, 4, 4, 2, 48, D), BF)
FOUR = pltpu.VMEM((4, BLOCK, D), BF)


def dma(*count):
    return pltpu.SemaphoreType.DMA(count)


def dot(left, right):
    return lax.dot_general(left, right, (((1,), (0,)), ((), ())), preferred_element_type=F32)


def dot_nt(left, right):
    return lax.dot_general(left, right, (((1,), (1,)), ((), ())), preferred_element_type=F32)


def dot_tn(left, right):
    return lax.dot_general(left, right, (((0,), (0,)), ((), ())), preferred_element_type=F32)


def norm_of(residual):
    centre = residual - jnp.mean(residual, axis=1, keepdims=True)
    scaled = lax.rsqrt(jnp.mean(centre * centre, axis=1, keepdims=True) + EPS)
    return centre * scaled, scaled


def norm_back(grad_out, normed, scaled, gain):
    grad_normed = grad_out * gain
    inner = (
        grad_normed
        - jnp.mean(grad_normed, axis=1, keepdims=True)
        - normed * jnp.mean(grad_normed * normed, axis=1, keepdims=True)
    )
    return (
        scaled * inner,
        jnp.sum(grad_out * normed, axis=0, keepdims=True),
        jnp.sum(grad_out, axis=0, keepdims=True),
    )


def head_masks():
    lane = lax.broadcasted_iota(jnp.int32, (BLOCK, 128), 1)
    return lane < 64


def vector_rows(vraw, out):
    groups = [vraw[yh, z][0:8, :256].astype(F32) for yh in range(2) for z in range(4)]
    values = jnp.concatenate(groups, axis=0).astype(BF)
    lane = lax.broadcasted_iota(jnp.int32, (64, D), 1)
    device = lax.broadcasted_iota(jnp.int32, (64, D), 0)

    def rows(start, width, count):
        found = []
        for r in range(count):
            spread = jnp.where(device == (lane + r * D) // width, 1.0, 0.0).astype(BF)
            wide = dot_tn(values[:, start : start + width], spread)
            entry = lax.broadcasted_iota(jnp.int32, wide.shape, 0)
            at = lax.broadcasted_iota(jnp.int32, wide.shape, 1) + r * D
            found.append(
                jnp.sum(jnp.where(entry == at % width, wide, 0.0), axis=0, keepdims=True)
            )
        return found

    found = rows(0, 24, 2)
    for start in (24, 36, 48):
        found += rows(start, 12, 1)
    found += rows(60, 48, 4)
    for start in (108, 120, 132):
        found += rows(start, 12, 1)
    out[...] = jnp.concatenate(found + [jnp.zeros((4, D), F32)], axis=0)


def column_sum(values):
    return jnp.sum(values.astype(F32), axis=0, keepdims=True)


def attention_forward(u, joined, vec, weights, qkv, probs, both, normed, scaled):
    q = ((dot(u, weights.get(0)) + vec[0:1]) * 0.125).astype(BF)
    k = dot(u, weights.get(1)).astype(BF)
    v = (dot(u, weights.get(2)) + vec[1:2]).astype(BF)
    qkv[0] = q
    qkv[1] = k
    qkv[2] = v
    low_half = head_masks()
    for pair in range(HEADS // 2):
        lanes = slice(pair * 128, pair * 128 + 128)
        q2, k2, v2 = q[:, lanes], k[:, lanes], v[:, lanes]
        outs = []
        for h in range(2):
            mine = low_half if h == 0 else jnp.logical_not(low_half)
            scores = dot_nt(jnp.where(mine, q2, jnp.zeros_like(q2)), k2)
            scores = jnp.where(joined, scores, -1e30)
            top = jnp.max(scores, axis=1, keepdims=True)
            exponent = jnp.exp(scores - top)
            total = jnp.sum(exponent, axis=1, keepdims=True)
            rows = (exponent / total).astype(BF)
            probs[2 * pair + h] = rows
            outs.append(dot(rows, v2))
        both[1, :, lanes] = jnp.where(low_half, outs[0], outs[1]).astype(BF)
    branch = dot(both[1], weights.get(3)) + vec[2:3]
    n1, s1 = norm_of(u.astype(F32) + branch)
    normed[...] = n1
    scaled[...] = jnp.broadcast_to(s1, (BLOCK, 128))
    return (n1 * vec[3:4] + vec[4:5]).astype(BF)


def ffn_forward(hidden, vec, expand, contract, act, slope, normed, scaled):
    for j in range(4):
        pre = dot(hidden, expand.get(j)) + vec[5 + j : 6 + j]
        half = 0.5 * (1.0 + lax.erf(pre * 0.7071067811865476))
        act[j] = (pre * half).astype(BF)
        slope[j] = (half + pre * jnp.exp(-0.5 * pre * pre) * 0.3989422804014327).astype(BF)
    total = hidden.astype(F32) + vec[9:10]
    for j in range(4):
        total = total + dot(act[j], contract.get(j))
    n2, s2 = norm_of(total)
    normed[...] = n2
    scaled[...] = jnp.broadcast_to(s2, (BLOCK, 128))
    return n2 * vec[10:11] + vec[11:12]


def ffn_backward(grad, vec, n2, s2, slope, expand, contract, vecs, dffn_ref, dpre_ref):
    dr2, dgain, dshift = norm_back(grad, n2[...], s2[:, 0:1], vec[10:11])
    dffn = dr2.astype(BF)
    dffn_ref[...] = dffn
    vecs[...] = jnp.zeros((16, D), F32)
    vecs[9:10] = column_sum(dffn)
    vecs[10:11] = dgain
    vecs[11:12] = dshift
    for j in range(4):
        dact = dot_nt(dffn, contract.get(j))
        dpre = (dact * slope[j].astype(F32)).astype(BF)
        dpre_ref[j] = dpre
        vecs[5 + j : 6 + j] = column_sum(dpre)
    total = dr2
    for j in range(4):
        total = total + dot_nt(dpre_ref[j], expand.get(j))
    return total


def attention_backward(dhidden, vec, n1, s1, qkv, probs, weights, vecs, parts, head):
    dr1, dgain, dshift = norm_back(dhidden, n1[...], s1[:, 0:1], vec[3:4])
    parts[3] = dr1.astype(BF)
    dattended = dot_nt(parts[3], weights.get(3)).astype(BF)
    low_half = head_masks()
    for pair in range(HEADS // 2):
        lanes = slice(pair * 128, pair * 128 + 128)
        q2, k2, v2 = qkv[0, :, lanes], qkv[1, :, lanes], qkv[2, :, lanes]
        do2 = dattended[:, lanes]
        dqs = []
        dk2 = jnp.zeros((BLOCK, 128), F32)
        dv2 = jnp.zeros((BLOCK, 128), F32)
        for h in range(2):
            mine = low_half if h == 0 else jnp.logical_not(low_half)
            do_h = jnp.where(mine, do2, jnp.zeros_like(do2))
            rows_low = probs[2 * pair + h]
            rows = rows_low.astype(F32)
            dprobs = dot_nt(do_h, v2)
            dscores = (
                rows * (dprobs - jnp.sum(rows * dprobs, axis=1, keepdims=True))
            ).astype(BF)
            dqs.append(dot(dscores, k2))
            dk2 = dk2 + dot_tn(dscores, jnp.where(mine, q2, jnp.zeros_like(q2)))
            dv2 = dv2 + dot_tn(rows_low, do_h)
        parts[0, :, lanes] = (jnp.where(low_half, dqs[0], dqs[1]) * 0.125).astype(BF)
        parts[1, :, lanes] = dk2.astype(BF)
        parts[2, :, lanes] = dv2.astype(BF)
    total = dr1
    for j in range(3):
        total = total + dot_nt(parts[j], weights.get(j))
    head[...] = jnp.concatenate(
        [column_sum(parts[0]), column_sum(parts[2]), column_sum(parts[3]), dgain, dshift, vecs[5:16]],
        axis=0,
    ).astype(BF)
    return total


def put_attention_inputs(out, both, xk, xs):
    core = lax.axis_index("core")
    for to, second in ((xk, core), (xs, 1 - core)):
        out.put(both.at[0], to.at[0])
        out.put(both.at[second], to.at[1])


def put_halves(out, four, one, keep, send):
    core = lax.axis_index("core")
    for to, half in ((keep, core), (send, 1 - core)):
        out.put(four.at[pl.ds(2 * half, 2)], to.at[pl.ds(0, 2)])
        out.put(one, to.at[2])


def wait_vectors(vraw, sems):
    for yh in range(2):
        for z in range(4):
            here = vraw.at[yh, z]
            pltpu.make_async_copy(here, here, sems.at[yh, z]).wait()


def fa_kernel(layer, u, sc, sr, *rest):
    pieces = rest[:16]
    hidden_o, n1_o, s1_o, qkv_o, probs_o, xk_o, xs_o, vec_o = rest[16:24]
    wa, vraw, hidden, n1, s1, qkv, probs, both, vec, sem_w, sem_v, sem_o = rest[24:]
    out = Out(sem_o)
    weights = attention_chunks(layer, pieces, wa, sem_w, vraw, sem_v)
    both[0] = u[...]
    wait_vectors(vraw, sem_v)
    vector_rows(vraw, vec)
    out.put(vec, vec_o)
    joined = sc[...] == sr[...]
    hidden[...] = attention_forward(u[...], joined, vec, weights, qkv, probs, both, n1, s1)
    for source, to in ((hidden, hidden_o), (n1, n1_o), (s1, s1_o), (qkv, qkv_o), (probs, probs_o)):
        out.put(source, to)
    put_attention_inputs(out, both, xk_o, xs_o)
    out.drain()


def ff_kernel(layer, hidden, vec, *rest):
    pieces, pieces_c = rest[:16], rest[16:18]
    result_o, n2_o, s2_o, slope_o, xk_o, xs_o = rest[18:24]
    we, wc, act, slope, n2, s2, result, sem_e, sem_c, sem_o = rest[24:]
    out = Out(sem_o)
    expand = expand_chunks(layer, pieces, we, sem_e)
    contract = Contract(layer, pieces_c, wc, sem_c)
    values = ffn_forward(hidden[...], vec, expand, contract, act, slope, n2, s2)
    put_halves(out, act, hidden, xk_o, xs_o)
    out.put(slope, slope_o)
    result[...] = values.astype(BF)
    for source, to in ((result, result_o), (n2, n2_o), (s2, s2_o)):
        out.put(source, to)
    out.drain()


def second_kernel(layer, keep, u, sc, sr, cot, *rest):
    pieces, pieces_c = rest[:16], rest[16:18]
    last_o, passed_o, xk_o, xs_o, dk_o, ds_o, xka_o, xsa_o, dka_o, dsa_o = rest[18:28]
    wa, we, wc, vraw, hidden, n1, s1, qkv, probs, both, vec = rest[28:39]
    act, slope, n2, s2, last, dpre, dffn, vecs, parts, head, passed = rest[39:50]
    sem_w, sem_v, sem_e, sem_c, sem_o = rest[50:]
    out = Out(sem_o)
    weights = attention_chunks(layer, pieces, wa, sem_w, vraw, sem_v)
    expand = expand_chunks(layer, pieces, we, sem_e)
    contract = Contract(layer, pieces_c, wc, sem_c)
    both[0] = u[...]
    wait_vectors(vraw, sem_v)
    vector_rows(vraw, vec)
    joined = sc[...] == sr[...]
    hidden[...] = attention_forward(u[...], joined, vec, weights, qkv, probs, both, n1, s1)
    put_attention_inputs(out, both, xka_o, xsa_o)
    values = ffn_forward(hidden[...], vec, expand, contract, act, slope, n2, s2)
    put_halves(out, act, hidden, xk_o, xs_o)
    kept = keep[0] > 9
    last[...] = jnp.where(kept, values.astype(BF), u[...])
    out.put(last, last_o)
    grad = jnp.where(kept, cot[...].astype(F32), 0.0)
    dhidden = ffn_backward(grad, vec, n2, s2, slope, expand, contract, vecs, dffn, dpre)
    put_halves(out, dpre, dffn, dk_o, ds_o)
    du = attention_backward(dhidden, vec, n1, s1, qkv, probs, weights, vecs, parts, head)
    put_attention_grads(out, parts, head, dka_o, dsa_o)
    passed[...] = jnp.where(kept, du.astype(BF), cot[...])
    out.put(passed, passed_o)
    out.drain()


def bf_kernel(layer, grad, vec, n2, s2, slope, *rest):
    pieces, pieces_c = rest[:16], rest[16:18]
    dhidden_o, vecs_o, dk_o, ds_o = rest[18:22]
    we, wc, dpre, dffn, dhidden, vecs, sem_e, sem_c, sem_o = rest[22:]
    out = Out(sem_o)
    contract = Contract(layer, pieces_c, wc, sem_c)
    expand = expand_chunks(layer, pieces, we, sem_e)
    dhidden[...] = ffn_backward(
        grad[...].astype(F32), vec, n2, s2, slope, expand, contract, vecs, dffn, dpre
    )
    put_halves(out, dpre, dffn, dk_o, ds_o)
    out.put(dhidden, dhidden_o)
    out.put(vecs, vecs_o)
    out.drain()


def put_attention_grads(out, parts, head, dk, ds):
    core = lax.axis_index("core")
    for to, half in ((dk, core), (ds, 1 - core)):
        for j in range(2):
            out.put(parts.at[2 * half + j], to.at[pl.ds(j * BLOCK, BLOCK), :])
        out.put(head, to.at[pl.ds(2 * BLOCK, 16), :])


def ba_kernel(layer, dhidden, vecs, vec, n1, s1, qkv, probs, *rest):
    pieces = rest[:16]
    du_o, dk_o, ds_o = rest[16:19]
    wa, parts, head, du, sem_w, sem_o = rest[19:]
    out = Out(sem_o)
    weights = attention_chunks(layer, pieces, wa, sem_w)
    du[...] = attention_backward(
        dhidden[...], vec, n1, s1, qkv, probs, weights, vecs, parts, head
    ).astype(BF)
    put_attention_grads(out, parts, head, dk_o, ds_o)
    out.put(du, du_o)
    out.drain()


def bring_rows(own, other, parts, to, sems, first):
    copies = []
    for i in range(parts):
        for r, ref in enumerate((own, other)):
            copies.append(
                pltpu.make_async_copy(
                    ref.at[i],
                    to.at[i, pl.ds(r * BLOCK, BLOCK), :],
                    sems.at[first + 2 * i + r],
                )
            )
    return copies


def bring_grads(own, other, to, head, sems, first):
    copies = []
    for i in range(2):
        for r, ref in enumerate((own, other)):
            copies.append(
                pltpu.make_async_copy(
                    ref.at[pl.ds(i * BLOCK, BLOCK), :],
                    to.at[i, pl.ds(r * BLOCK, BLOCK), :],
                    sems.at[first + 2 * i + r],
                )
            )
    for r, ref in enumerate((own, other)):
        copies.append(
            pltpu.make_async_copy(
                ref.at[pl.ds(2 * BLOCK, 16), :], head.at[r], sems.at[first + 4 + r]
            )
        )
    return copies


def wait_all(copies):
    for copy in copies:
        copy.wait()


def slab_rows(scratch, which, blocks):
    rows = [scratch[pl.ds(pl.multiple_of(b * ROWS + which * 24, 8), 24), :] for b in blocks]
    return jnp.concatenate(rows, axis=0).astype(BF)


def w1_kernel(xk, xr, dk, dr, xka, xra, dka, dra, result, x, d, xa, da, head, grad, staged, sem_i, sem_o):
    d_in, x_in = bring_rows(dk, dr, 3, d, sem_i, 0), bring_rows(xk, xr, 3, x, sem_i, 6)
    xa_in, da_in = bring_rows(xka, xra, 2, xa, sem_i, 12), bring_grads(dka, dra, da, head, sem_i, 16)
    for copy in d_in[4:6] + x_in + d_in[:4] + xa_in + da_in:
        copy.start()
    out = Out(sem_o)
    wait_all(d_in[4:6])
    for a in range(2):
        wait_all(x_in[2 * a : 2 * a + 2])
        values = dot_tn(x[a], d[2]).astype(BF)
        for b in range(8):
            staged[a * 8 + b, 0:96] = values[b * ROWS : (b + 1) * ROWS]
    out.put(staged.at[:, pl.ds(0, 96), :], result.at[:, pl.ds(0, 96), :])

    def both_yh(first):
        for z in range(4):
            for xs in range(4):
                staged[z * 4 + xs, first : first + 48] = slab_rows(grad, xs, (z, 4 + z))

    wait_all(x_in[4:6] + d_in[:4])
    for a in range(2):
        grad[...] = dot_tn(x[2], d[a])
        both_yh(96 + 48 * a)
    out.put(staged.at[:, pl.ds(96, 96), :], result.at[:, pl.ds(96, 96), :])
    wait_all(xa_in + da_in)
    for a in range(2):
        grad[...] = dot_tn(xa[a], da[a])
        both_yh(192 + 48 * a)
    vec = (head[0].astype(F32) + head[1].astype(F32)).astype(BF)
    for b in range(16):
        staged[b, 288:304] = vec
    out.put(staged.at[:, pl.ds(192, 112), :], result.at[:, pl.ds(192, 112), :])
    out.drain()


def wf_kernel(xk, xr, dk, dr, *rest):
    outs_c, outs_b = rest[:4], rest[4:8]
    x, d, grad, staged, sem_i, sem_o = rest[8:]
    d_in, x_in = bring_rows(dk, dr, 3, d, sem_i, 0), bring_rows(xk, xr, 3, x, sem_i, 6)
    for copy in d_in[4:6] + x_in + d_in[:4]:
        copy.start()
    out = Out(sem_o)
    wait_all(d_in[4:6])
    for a in range(2):
        here = slice(a * 192, (a + 1) * 192)
        wait_all(x_in[2 * a : 2 * a + 2])
        grad[...] = dot_tn(x[a], d[2])
        for k in range(4):
            staged[k, here] = slab_rows(grad, lax.rem(position(Y) + k, 4), range(8))
    for k in range(4):
        out.put(staged.at[k], outs_c[k])
    wait_all(x_in[4:6] + d_in[:4])
    for a in range(2):
        here = slice(a * 192, (a + 1) * 192)
        grad[...] = dot_tn(x[2], d[a])
        for k in range(4):
            staged[4 + k, here] = slab_rows(grad, lax.rem(position("x") + k, 4), range(8))
    for k in range(4):
        out.put(staged.at[4 + k], outs_b[k])
    out.drain()


def wa_kernel(xka, xra, dka, dra, *rest):
    outs = rest[:4]
    xa, da, head, grad, staged, sem_i, sem_o = rest[4:]
    xa_in, da_in = bring_rows(xka, xra, 2, xa, sem_i, 0), bring_grads(dka, dra, da, head, sem_i, 4)
    for copy in xa_in + da_in:
        copy.start()
    out = Out(sem_o)
    wait_all(xa_in + da_in)
    vec = (head[0].astype(F32) + head[1].astype(F32)).astype(BF)
    for a in range(2):
        grad[a] = dot_tn(xa[a], da[a]).astype(BF)
    for k in range(4):
        zs = lax.rem(position("z") + k, 4)
        for a in range(2):
            for yh in range(2):
                row = pl.multiple_of((yh * 4 + zs) * ROWS, ROWS)
                staged[k, (a * 2 + yh) * ROWS : (a * 2 + yh + 1) * ROWS] = grad[a, pl.ds(row, ROWS), :]
        staged[k, 384:400] = vec
        out.put(staged.at[k], outs[k])
    out.drain()


def pack_kernel(iw, ib, ow, ob, fg, fs, ew, eb, cw, cb, sg, ss, own, contract, scratch):
    scratch[96:104] = jnp.zeros((8, D), F32)
    for j in range(8):
        rows = iw[0, :, j * D : (j + 1) * D] if j < 3 else ow[0]
        if j > 3:
            rows = ew[0, :, (j - 4) * D : (j - 3) * D]
        scratch[j * 12 : (j + 1) * 12] = rows
    start = 0
    for ref in (ib, ob, fg, fs, eb, cb, sg, ss):
        width = ref.shape[1]
        scratch[96:97, start : start + width] = ref[...]
        start += width
    own[...] = scratch[...].astype(BF)
    contract[...] = cw[0].astype(BF)


def shape(*dims, dtype=F32):
    return jax.ShapeDtypeStruct(dims, dtype)


def call(kernel, outs, args, in_hbm=0, scratch=(), name="kernel", outs_hbm=True, smem=0, flops=1000):
    here = len(args) - in_hbm - smem
    in_specs = [pl.BlockSpec(memory_space=pltpu.SMEM)] * smem
    in_specs += [pl.BlockSpec(memory_space=pltpu.VMEM)] * here
    in_specs += [pl.BlockSpec(memory_space=pl.ANY)] * in_hbm
    out_space = pl.ANY if outs_hbm else pltpu.VMEM
    return pl.pallas_call(
        kernel,
        out_shape=outs,
        in_specs=in_specs,
        out_specs=[pl.BlockSpec(memory_space=out_space)] * len(outs),
        scratch_shapes=list(scratch),
        compiler_params=pltpu.CompilerParams(vmem_limit_bytes=56 * 1024 * 1024),
        cost_estimate=pl.CostEstimate(flops=flops, bytes_accessed=1024, transcendentals=0),
        name=name,
    )(*args)


ROWS_BF = shape(BLOCK, D, dtype=BF)
ROWS_F32 = shape(BLOCK, D)
SCALE = shape(BLOCK, 128)
QKV = shape(3, BLOCK, D, dtype=BF)
PROBS = shape(HEADS, BLOCK, BLOCK, dtype=BF)
SLOPE = shape(4, BLOCK, D, dtype=BF)
TWO = shape(2, BLOCK, D, dtype=BF)
THREE = shape(3, BLOCK, D, dtype=BF)
VECS = shape(16, D)
DA = shape(528, D, dtype=BF)


def vmem(*shapes):
    return [pltpu.VMEM(each.shape, each.dtype) for each in shapes]


HEAD_BF = shape(16, D, dtype=BF)
VRAW = shape(2, 4, 16, D, dtype=BF)


def first_attention(u, seg, pieces):
    saved = [ROWS_F32, SCALE, QKV, PROBS]
    return call(
        lambda *refs: fa_kernel(0, *refs),
        [ROWS_BF, *saved, TWO, TWO, VECS],
        [u, seg[:, None], seg[None, :], *pieces],
        16,
        [WA, *vmem(VRAW, ROWS_BF, *saved, TWO, VECS), dma(4, 8), dma(2, 4), dma(16)],
        name="attention_forward_0",
        flops=12_000_000_000,
    )


def first_ffn(hidden, vec, pieces, pieces_c):
    return call(
        lambda *refs: ff_kernel(0, *refs),
        [ROWS_BF, ROWS_F32, SCALE, SLOPE, THREE, THREE],
        [hidden, vec, *pieces, *pieces_c],
        18,
        [WA, WC, FOUR, *vmem(SLOPE, ROWS_F32, SCALE, ROWS_BF), dma(4, 8), dma(4, 2, 4), dma(16)],
        name="ffn_forward_0",
    )


def second_layer(depth, u, seg, cot, pieces, pieces_c):
    return call(
        lambda *refs: second_kernel(1, *refs),
        [ROWS_BF, ROWS_BF, THREE, THREE, THREE, THREE, TWO, TWO, DA, DA],
        [depth, u, seg[:, None], seg[None, :], cot, *pieces, *pieces_c],
        18,
        [WA, WA, WC, *vmem(VRAW, ROWS_BF, ROWS_F32, SCALE, QKV, PROBS, TWO, VECS)]
        + [FOUR, *vmem(SLOPE, ROWS_F32, SCALE, ROWS_BF)]
        + [FOUR, *vmem(ROWS_BF, VECS), FOUR, *vmem(HEAD_BF, ROWS_BF)]
        + [dma(4, 8), dma(2, 4), dma(4, 8), dma(4, 2, 4), dma(24)],
        name="second_layer",
        smem=1,
    )


def first_ffn_backward(grad, vec, n2, s2, slope, pieces, pieces_c):
    return call(
        lambda *refs: bf_kernel(0, *refs),
        [ROWS_F32, VECS, THREE, THREE],
        [grad, vec, n2, s2, slope, *pieces, *pieces_c],
        18,
        [WA, WC, FOUR, *vmem(ROWS_BF, ROWS_F32, VECS), dma(4, 8), dma(4, 2, 4), dma(16)],
        name="ffn_backward_0",
    )


def first_attention_backward(dhidden, vecs, vec, n1, s1, qkv, probs, pieces):
    return call(
        lambda *refs: ba_kernel(0, *refs),
        [ROWS_BF, DA, DA],
        [dhidden, vecs, vec, n1, s1, qkv, probs, *pieces],
        16,
        [WA, FOUR, *vmem(HEAD_BF, ROWS_BF), dma(4, 8), dma(16)],
        name="attention_backward_0",
    )


def both_cores(parts):
    return pltpu.VMEM((parts, 2 * BLOCK, D), BF)


def second_weights(args):
    return call(
        w1_kernel,
        [shape(16, 304, D, dtype=BF)],
        args,
        8,
        [both_cores(3), both_cores(3), both_cores(2), both_cores(2), pltpu.VMEM((2, 16, D), BF)]
        + [pltpu.VMEM((D, D), F32), pltpu.VMEM((16, 304, D), BF), dma(24), dma(4)],
        name="weights_1",
    )[0]


def first_ffn_weights(args):
    outs = call(
        wf_kernel,
        [shape(384, D, dtype=BF)] * 8,
        args,
        4,
        [both_cores(3), both_cores(3), pltpu.VMEM((D, D), F32)]
        + [pltpu.VMEM((8, 384, D), BF), dma(12), dma(8)],
        name="ffn_weights_0",
    )
    return outs[:4], outs[4:]


def first_attention_weights(args):
    return call(
        wa_kernel,
        [shape(400, D, dtype=BF)] * 4,
        args,
        4,
        [both_cores(2), both_cores(2), pltpu.VMEM((2, 16, D), BF), pltpu.VMEM((2, D, D), BF)]
        + [pltpu.VMEM((4, 400, D), BF), dma(10), dma(4)],
        name="attention_weights_0",
    )


def gather_first(masters):
    core = lax.axis_index("core")
    own, contract = call(
        pack_kernel,
        [shape(104, D, dtype=BF), shape(48, D, dtype=BF)],
        list(masters),
        0,
        [pltpu.VMEM((104, D), F32)],
        name="pack",
        outs_hbm=False,
    )
    own, contract = from_behind(own, "x"), from_behind(contract, Y)
    contract, own = lax.optimization_barrier((contract, own))
    contract, along_x = by_position(contract, position(Y)), by_position(own, position("x"))
    contract = lax.all_gather(contract, "z", axis=0)
    other = swap_core(along_x)
    first, second = jnp.where(core == 0, along_x, other), jnp.where(core == 0, other, along_x)
    both = jnp.stack([first, second])
    chunks = both[:, :, :96].reshape(2, 4, 8, 12, D).transpose(2, 1, 0, 3, 4).reshape(8, ROWS, D)
    vector = both[:, :, 96].transpose(1, 0, 2).reshape(8, D)
    chunks = lax.dynamic_slice_in_dim(chunks, 4 * core, 4, 0).reshape(384, D)
    load = jnp.concatenate([chunks, vector, jnp.zeros((8, D), BF)], axis=0)
    load = [load] + [ahead_crossed(load, k, 0) for k in (1, 2, 3)]
    load, contract = lax.optimization_barrier((load, contract))
    contract = lax.all_gather(contract, "x", axis=0)
    load = by_position(load, jnp.where(core == 0, position(Y), position("z")))
    return load.reshape(2, 2, 400, D), contract


def gather_forward(masters, u, seg):
    load, contract = gather_first(masters)
    own = []
    for half in range(2):
        value = load[:, half]
        own.append([value] + [ahead_crossed(value, k, 1) for k in (1, 2, 3)])
    other = [[swap_core(piece) for piece in own[0]]]
    attended = list(first_attention(u, seg, own[0] + own[1][:1] * 4 + other[0] + own[1][:1] * 4))
    attended[0], contract, own[1][0] = lax.optimization_barrier(
        (attended[0], contract, own[1][0])
    )
    other_c, early = swap_core(contract), swap_core(own[1][0])
    own[1][1:], other_c, early = lax.optimization_barrier((own[1][1:], other_c, early))
    other.append([early] + [swap_core(piece) for piece in own[1][1:]])
    return own[0] + own[1] + other[0] + other[1], [contract, other_c], attended


def summed(pieces):
    total = pieces[0].astype(F32)
    for piece in pieces[1:]:
        total = total + piece.astype(F32)
    return total


def scatter_ahead(pieces, axis):
    return [pieces[0]] + [ahead(pieces[k], axis, k) for k in (1, 2, 3)]


def pieces_ahead(parts, axis):
    here = position(axis)
    return [lax.dynamic_index_in_dim(parts, (here + k) % 4, 0, keepdims=False) for k in range(4)]


def reduce_along(parts, axis):
    return summed(scatter_ahead(pieces_ahead(parts, axis), axis))


def reduce_last(attention, expand, contract, second):
    section, core = lax.axis_index("section"), lax.axis_index("core")
    a, b, c = summed(attention), summed(expand), summed(contract)
    vec = a[384:]
    a, b = a[:384].reshape(2, 2, ROWS, D), b.reshape(2, 2, ROWS, D)
    blocks = []
    for yh in range(2):
        for slot in range(2):
            parts = [a[slot, yh], vec, b[slot, yh]]
            blocks.append(jnp.concatenate([part.astype(BF) for part in parts], axis=0))
    along_y = reduce_along(jnp.stack(blocks), Y)
    c = reduce_along(c.astype(BF).reshape(4, ROWS, D), "z")
    b = reduce_along(along_y[112:].astype(BF).reshape(4, 24, D), "z")

    def by_x(rows):
        return rows.astype(BF).reshape(4, 24, D)

    vec = jnp.broadcast_to(along_y[96:112].astype(BF)[None], (4, 16, D))
    load = reduce_along(jnp.concatenate([by_x(along_y[:96]), by_x(c), vec], axis=1), "x")
    a0, c0 = load[:24], load[24:48]
    second_b, second_a = second[96:192].reshape(2, 2, 24, D), second[192:288].reshape(2, 2, 24, D)
    blocks = []
    for yh in range(2):
        for slot in range(2):
            y = 2 * yh + slot
            parts = [second[24 * y : 24 * y + 24], second_b[slot, yh], second_a[slot, yh]]
            blocks.append(jnp.concatenate(parts + [second[288:]], axis=0))
    along_y = reduce_along(jnp.stack(blocks), Y)
    c1, b1, a1, vec1 = along_y[:24], along_y[24:48], along_y[48:72], along_y[72:]
    vec = jnp.where(section == 0, load[48:], vec1)
    mine = jnp.where(section == 0, jnp.stack([a0, b, c0]), jnp.stack([a1, b1, c1]))
    others = jnp.where(section == 0, jnp.stack([a1, b1, c1]), jnp.stack([a0, b, c0]))
    near, far = crossed_owner(mine[2], False), crossed_owner(others[2], True)
    contract = jnp.concatenate(
        [jnp.where(section == 0, near, far), jnp.where(section == 0, far, near)]
    )
    mine, others = mine[:2].reshape(2, 2, 12, D), others[:2].reshape(2, 2, 12, D)

    def rows_of(value, which):
        return lax.dynamic_index_in_dim(value, which, 1, keepdims=False)

    here = rows_of(mine, core)
    near = to_neighbour(rows_of(mine, 1 - core), False, True)
    far = to_neighbour(rows_of(others, core), True, False)
    far_near = to_neighbour(rows_of(others, 1 - core), True, True)
    own, other = jnp.stack([here, far]), jnp.stack([near, far_near])
    low, high = jnp.where(core == 0, own, other), jnp.where(core == 0, other, own)
    flip = section == 0
    chunks = [jnp.where(flip, low[0], low[1]), jnp.where(flip, low[1], low[0])]
    chunks += [jnp.where(flip, high[0], high[1]), jnp.where(flip, high[1], high[0])]
    input_weight = jnp.concatenate([chunks[j][0] for j in range(3)], axis=1)
    expand_weight = jnp.concatenate([chunks[j][1] for j in range(4)], axis=1)
    return input_weight, chunks[3][0], expand_weight, contract, vec


def to_neighbour(value, other_section, other_core):
    pairs = []
    for s in range(2):
        for c in range(2):
            to = (1 - s if other_section else s) * 2 + (1 - c if other_core else c)
            pairs.append((s * 2 + c, to))
    return lax.ppermute(value, ("section", "core"), pairs)


def crossed_owner(value, other_section):
    pairs = []
    for s in range(2):
        for yh in range(2):
            for c in range(2):
                to = 1 - s if other_section else s
                pairs.append(((s * 2 + yh) * 2 + c, (to * 2 + c) * 2 + yh))
    return lax.ppermute(value, ("section", "yh", "core"), pairs)


def on_device(tokens, segment_ids, depth, *rest):
    masters = rest[:12]
    cotangent = rest[12]
    section = lax.axis_index("section")
    place = (
        lax.axis_index("yh") * 32
        + lax.axis_index("z") * 8
        + lax.axis_index("x") * 2
        + lax.axis_index("core")
    )
    u = lax.dynamic_slice_in_dim(tokens, section * BLOCK, BLOCK, 0)
    seg = lax.dynamic_slice_in_dim(segment_ids, section * BLOCK, BLOCK, 0)
    cot = lax.dynamic_slice_in_dim(cotangent, section * BLOCK, BLOCK, 0)

    def halves(of_first, of_second):
        mine = jnp.where(section == 0, of_first, of_second)
        theirs = ahead(jnp.where(section == 0, of_second, of_first), "section", 1)
        return jnp.concatenate(
            [jnp.where(section == 0, mine, theirs), jnp.where(section == 0, theirs, mine)]
        )[None]

    pieces, pieces_c, attended = gather_forward(masters, u, seg)
    hidden, *saved0, xka0, xsa0, vec0 = attended
    middle, n2_0, s2_0, slope0, xk0, xs0 = first_ffn(hidden, vec0, pieces, pieces_c)
    last, passed, xk1, xs1, dk1, ds1, xka1, xsa1, dka1, dsa1 = second_layer(
        depth, middle, seg, cot, pieces, pieces_c
    )
    dhidden, vecs, dk0, ds0 = first_ffn_backward(
        passed, vec0, n2_0, s2_0, slope0, pieces, pieces_c
    )
    received = [swap_core(each) for each in (xs1, ds1, xsa1, dsa1)]
    dhidden, received = lax.optimization_barrier((dhidden, received))
    weights1 = second_weights(
        [xk1, received[0], dk1, received[1], xka1, received[2], dka1, received[3]]
    )
    dhidden, weights1 = lax.optimization_barrier((dhidden, weights1))
    weights1 = weights1.reshape(16 * 304, D)
    second = lax.psum_scatter(weights1, ("z", "x"), scatter_dimension=0, tiled=True)
    first, dka0, dsa0 = first_attention_backward(dhidden, vecs, vec0, *saved0, pieces)
    received = [swap_core(each) for each in (xs0, ds0, xsa0)]
    first, received = lax.optimization_barrier((first, received))
    contract0, expand0 = first_ffn_weights([xk0, received[0], dk0, received[1]])
    received_a = swap_core(dsa0)
    contract0, expand0, received_a = lax.optimization_barrier((contract0, expand0, received_a))
    attention0 = first_attention_weights([xka0, received[2], dka0, received_a])
    attention0 = scatter_ahead(attention0, "z")
    contract0 = scatter_ahead(contract0, Y)
    expand0 = scatter_ahead(expand0, "x")
    layer_outputs = halves(middle, last)
    input_grads = halves(first, passed)
    iw, ow, ew, cw, vec = reduce_last(attention0, expand0, contract0, second)

    def shard(first_row, rows, width):
        flat = vec[first_row : first_row + rows].reshape(-1)
        return lax.dynamic_slice_in_dim(flat, place * width, width, 0)[None]

    return (
        layer_outputs,
        input_grads,
        iw[None],
        shard(0, 2, 24),
        ow[None],
        shard(2, 1, 12),
        shard(3, 1, 12),
        shard(4, 1, 12),
        ew[None],
        shard(5, 4, 48),
        cw[None],
        shard(9, 1, 12),
        shard(10, 1, 12),
        shard(11, 1, 12),
    )


def solution(mesh):
    wide = Mesh(mesh.devices.reshape(2, 2, 4, 4, 2), ("section", "yh", "z", "x", "core"))
    dp = ("yh", "z", "x", "core")
    matrix, vector = P("section", dp, None), P("section", dp)
    rows = P(dp, None)
    weights = (
        matrix,
        vector,
        matrix,
        vector,
        vector,
        vector,
        matrix,
        vector,
        matrix,
        vector,
        vector,
        vector,
    )
    return jax.shard_map(
        on_device,
        mesh=wide,
        in_specs=(rows, P(dp), P(dp)) + weights + (rows,),
        out_specs=(matrix, matrix) + weights,
        check_vma=False,
    )
```

time: 1550 us -> 388 us (0.25)
  blocking collectives: 906 us -> 0 us
  matrix products: 144 us -> 0 us
  waiting for transfers between devices: 20.9 us -> 152 us
  local copies, waits for them, and re-layouts: 146 us -> 25.7 us
  starting transfers between devices: 199 us -> 89.2 us
  Pallas kernels: 0 us -> 92.7 us
  other arithmetic: 90 us -> 6.13 us
    unnamed x2 -> x0, blocking collectives: 581 us -> none
    all_gather x1 -> x0, blocking collectives: 325 us -> none  [on_device(): lax.all_gather(low_masters[1], 'dp', axis=0, tiled=True)]
    unnamed x48 -> x0, starting transfers between devices: 188 us -> none
    ppermute x6 -> x64, waiting for transfers between devices: 15.8 us -> 150 us  [the longest x50 85.7 us: ahead(): lax.ppermute(value, axis, [(at[i], at[(i + steps) % count]) for i in rang...]
    dot_general x42 -> x0, matrix products: 129 us -> none  [the longest x8 32.3 us: weight_grad(): jnp.einsum('rk,rn->kn', left, right, preferred_element_type=jnp.float32)]
    pallas_call x0 -> x9, Pallas kernels: none -> 92.7 us  [call(): pl.pallas_call(kernel, out_shape=outs, in_specs=in_specs, out_specs=[pl.B...]
    unnamed x121 -> x98, local copies, waits for them, and re-layouts: 104 us -> 13.8 us
    ppermute x6 -> x64, starting transfers between devices: 10.6 us -> 89.1 us  [the longest x50 68.9 us: ahead(): lax.ppermute(value, axis, [(at[i], at[(i + steps) % count]) for i in rang...]
  transfers between devices with their start and end apart: 59 -> 67, of which waited for: 6 -> 37; matrix products, arithmetic and copies ran while one was open for 30% -> 5% of each run, Pallas kernels for 0% -> 13%
where the time goes in v1:
time: 388 us; the launch traced here: 381 us
  waiting for transfers between devices  152 us (39%)
  Pallas kernels  92.7 us (24%)
  starting transfers between devices  89.2 us (23%)
  local copies, waits for them, and re-layouts  25.7 us (7%)
  between operations  15.7 us (4%)
  other arithmetic  6.13 us (2%)
    pallas_call x9, Pallas kernels, call(): pl.pallas_call(kernel, out_shape=outs, in_specs=in_specs, out_specs=[pl.B...  92.7 us
    ppermute x50, waiting for transfers between devices, ahead(): lax.ppermute(value, axis, [(at[i], at[(i + steps) % count]) for i in rang...  85.7 us
    ppermute x50, starting transfers between devices, ahead(): lax.ppermute(value, axis, [(at[i], at[(i + steps) % count]) for i in rang...  68.9 us
    ppermute x9, waiting for transfers between devices, ahead_crossed(): return lax.ppermute(value, ('section', 'yh', 'z', 'core'), pairs)  63.5 us
    unnamed x98, local copies, waits for them, and re-layouts  13.8 us
    ppermute x9, starting transfers between devices, ahead_crossed(): return lax.ppermute(value, ('section', 'yh', 'z', 'core'), pairs)  11.9 us
  transfers between devices with their start and end apart: 67, of which 37 were waited for; matrix products, arithmetic and copies ran while one was open for 5% of the time, Pallas kernels for 13%

profile of v1, /device:TPU:1, one launch (start us, length us, event | category | flops | bytes accessed | tf_op | source)
XLA Modules:
  0.0 381.0 jit_solution(12997561869966567696)
XLA Ops:
  11.9 1.9 pack.1
  13.8 2.0 collective-permute-start.3
  15.9 2.5 collective-permute-start.4
  20.8 2.6 collective-permute-start.1
  26.4 1.7 collective-permute-done.2
  31.2 4.0 %collective-permute-start.6 = (bf16[4,104,768]{2,1,0:T(8,128)(2,1)S(1)}, bf16[4,104,768]{2,1,0:T(8,128)(2,1)S(1)}, u32[]{:S(2)}, u32[]{:S(2)}) collective-permute-start(bf16[4,104,768]{2,1,0:T(8,128)(2,1)S(1)} %constant_dynamic-slice_fusion.10), channel_id=1, source_target_pairs={{0,1},{1,0},{2,3},{3,2},{4,5},{5,4},{6,7},{7,6},{8,9},{9,8},{10,11... | collective-permute-start | bytes 1916936 | tf_op jit(solution)/shard_map/ppermute | solution.py:31
  40.7 3.3 collective-permute-start.8
  44.8 10.2 %collective-permute-done.7 = bf16[400,768]{1,0:T(8,128)(2,1)S(1)} collective-permute-done((bf16[400,768]{1,0:T(8,128)(2,1)S(1)}, bf16[400,768]{1,0:T(8,128)(2,1)S(1)}, u32[]{:S(2)}, u32[]{:S(2)}) %collective-permute-start.7) | collective-permute-done | bytes 614432 | tf_op jit(solution)/shard_map/ppermute | solution.py:55
  55.0 12.7 %collective-permute-done.8 = bf16[400,768]{1,0:T(8,128)(2,1)S(1)} collective-permute-done((bf16[400,768]{1,0:T(8,128)(2,1)S(1)}, bf16[400,768]{1,0:T(8,128)(2,1)S(1)}, u32[]{:S(2)}, u32[]{:S(2)}) %collective-permute-start.8) | collective-permute-done | bytes 614432 | tf_op jit(solution)/shard_map/ppermute | solution.py:55
  71.3 2.8 collective-permute-start.11
  75.1 13.4 %collective-permute-done.10.refs_4_.refs_3_.refs_6_.refs_8_ = bf16[2,400,768]{2,1,0:T(8,128)(2,1)S(1)} collective-permute-done((bf16[2,400,768]{2,1,0:T(8,128)(2,1)S(1)}, bf16[2,400,768]{2,1,0:T(8,128)(2,1)S(1)}, u32[]{:S(2)}, u32[]{:S(2)}) %collective-permute-start.10) | collective-permute-done | bytes 1228832 | tf_op jit(solution)/shard_map/ppermute | solution.py:55
  88.5 14.5 %collective-permute-start.14 = (bf16[2,400,768]{2,1,0:T(8,128)(2,1)S(1)}, bf16[2,400,768]{2,1,0:T(8,128)(2,1)}, u32[]{:S(2)}, u32[]{:S(2)}) collective-permute-start(bf16[2,400,768]{2,1,0:T(8,128)(2,1)S(1)} %collective-permute-done.10.refs_4_.refs_3_.refs_6_.refs_8_), channel_id=1, source_target_pairs={{0,1},{1,0},{2,3},{3,2},{4,5},{5,4},{6,7},{7,6},{8,9},{9,8},{10,11... | collective-permute-start | bytes 3686408 | tf_op jit(solution)/shard_map/ppermute | solution.py:31
  107.6 1.8 collective-permute-done.16.refs_14_.refs_13_.refs_16_.refs_18_
  109.4 11.5 %attention_forward_0.1 = (bf16[256,768]{1,0:T(8,128)(2,1)}, f32[256,768]{1,0:T(8,128)}, f32[256,128]{1,0:T(8,128)}, bf16[3,256,768]{2,1,0:T(8,128)(2,1)}, bf16[1...) custom-call(bf16[256,768]{1,0:T(8,128)(2,1)} %constant_dynamic-slice_f, ...), custom_call_target="tpu_custom_call" | custom-call | flops 12000000000 | bytes 1024 | tf_op jit(solution)/shard_map/attention_forward_0/pallas_call | solution.py:616
  121.4 2.8 collective-permute-start.18
  125.2 13.3 %collective-permute-done.17.refs_7_.refs_10_.refs_12_ = bf16[2,400,768]{2,1,0:T(8,128)(2,1)S(1)} collective-permute-done((bf16[2,400,768]{2,1,0:T(8,128)(2,1)S(1)}, bf16[2,400,768]{2,1,0:T(8,128)(2,1)S(1)}, u32[]{:S(2)}, u32[]{:S(2)}) %collective-permute-start.17) | collective-permute-done | bytes 1228832 | tf_op jit(solution)/shard_map/ppermute | solution.py:55
  138.5 13.0 %collective-permute-done.18.refs_8_.refs_11_.refs_13_ = bf16[2,400,768]{2,1,0:T(8,128)(2,1)S(1)} collective-permute-done((bf16[2,400,768]{2,1,0:T(8,128)(2,1)S(1)}, bf16[2,400,768]{2,1,0:T(8,128)(2,1)S(1)}, u32[]{:S(2)}, u32[]{:S(2)}) %collective-permute-start.18) | collective-permute-done | bytes 1228832 | tf_op jit(solution)/shard_map/ppermute | solution.py:55
  156.2 1.8 collective-permute-done.23.refs_16_.refs_19_.refs_21_
  158.0 1.8 collective-permute-done.24.refs_17_.refs_20_.refs_22_
  160.7 10.8 %ffn_forward_0.1 = (bf16[256,768]{1,0:T(8,128)(2,1)}, f32[256,768]{1,0:T(8,128)}, f32[256,128]{1,0:T(8,128)}, bf16[4,256,768]{2,1,0:T(8,128)(2,1)}, bf16[3,256,7...) custom-call(bf16[256,768]{1,0:T(8,128)(2,1)} %get-tuple-element.116.refs_0_, ...), custom_call_target="tpu_custom_call" | custom-call | flops 1000 | bytes 1024 | tf_op jit(solution)/shard_map/ffn_forward_0/pallas_call | solution.py:616
  171.5 24.2 %second_layer.1 = (bf16[256,768]{1,0:T(8,128)(2,1)}, bf16[256,768]{1,0:T(8,128)(2,1)}, bf16[3,256,768]{2,1,0:T(8,128)(2,1)}, bf16[3,256,768]{2,1,0:T(8,128)(2,1)...) custom-call(s32[1]{0:T(128)S(6)} %copy.128.refs_0_, ...), custom_call_target="tpu_custom_call" | custom-call | flops 1000 | bytes 1024 | tf_op jit(solution)/shard_map/second_layer/pallas_call | solution.py:616
  196.9 11.4 %ffn_backward_0.1 = (f32[256,768]{1,0:T(8,128)}, f32[16,768]{1,0:T(8,128)}, bf16[3,256,768]{2,1,0:T(8,128)(2,1)}, bf16[3,256,768]{2,1,0:T(8,128)(2,1)}) custom-call(bf16[256,768]{1,0:T(8,128)(2,1)} %get-tuple-element.127.refs_0_, f32[16,768]{1,0:T(8,128)} %get-tuple-element.117.refs_1_.refs_2_, f32[256,768]{1,0:T(8,128)} %get-tuple-element.128.refs_2_, ...), custom_call_target="tpu_custom_call" | custom-call | flops 1000 | bytes 1024 | tf_op jit(solution)/shard_map/ffn_backward_0/pallas_call | solution.py:616
  210.2 8.1 %weights_1.1 = bf16[16,304,768]{2,1,0:T(8,128)(2,1)} custom-call(bf16[3,256,768]{2,1,0:T(8,128)(2,1)} %get-tuple-element.137.xk, bf16[3,256,768]{2,1,0:T(8,128)(2,1)} %copy-done.17, bf16[3,256,768]{2,1,0:T(8,128)(2,1)} %get-tuple-element.139.dk, bf16[3,256,768]{2,1,0:T(8,128)(2,1)} %copy-done.18, bf16[2,256,768]{2,1,0:T(8,128)(2,1)} %get-tuple-element.141.xka, ...), custom_call_target="tpu_custom_call" | custom-call | flops 1000 | bytes 1024 | tf_op jit(solution)/shard_map/weights_1/pallas_call | solution.py:616
  218.9 12.2 %attention_backward_0.1 = (bf16[256,768]{1,0:T(8,128)(2,1)}, bf16[528,768]{1,0:T(8,128)(2,1)}, bf16[528,768]{1,0:T(8,128)(2,1)}) custom-call(f32[256,768]{1,0:T(8,128)} %get-tuple-element.145.refs_0_, f32[16,768]{1,0:T(8,128)} %get-tuple-element.146.refs_1_, f32[16,768]{1,0:T(8,128)} %get-tuple-element.117.refs_1_.refs_2_, ...), custom_call_target="tpu_custom_call" | custom-call | flops 1000 | bytes 1024 | tf_op jit(solution)/shard_map/attention_backward_0/pallas_call | solution.py:616
  232.8 2.2 collective-permute-done.32.xra
  236.5 7.5 %ffn_weights_0.1 = (bf16[384,768]{1,0:T(8,128)(2,1)}, bf16[384,768]{1,0:T(8,128)(2,1)}, bf16[384,768]{1,0:T(8,128)(2,1)}, bf16[384,768]{1,0:T(8,128)(2,1)}, bf16...) custom-call(bf16[3,256,768]{2,1,0:T(8,128)(2,1)} %get-tuple-element.159.xk, ...), custom_call_target="tpu_custom_call" | custom-call | flops 1000 | bytes 1024 | tf_op jit(solution)/shard_map/ffn_weights_0/pallas_call | solution.py:616
  245.1 2.9 collective-permute-start.45
  250.1 15.6 %collective-permute-done.33 = bf16[256,768]{1,0:T(8,128)(2,1)S(1)} collective-permute-done((bf16[256,768]{1,0:T(8,128)(2,1)S(1)}, bf16[256,768]{1,0:T(8,128)(2,1)S(1)}, u32[]{:S(2)}, u32[]{:S(2)}) %collective-permute-start.33) | collective-permute-done | bytes 393248 | tf_op jit(solution)/shard_map/ppermute | solution.py:31
  265.6 1.8 collective-permute-start.39
  268.8 5.0 %attention_weights_0.1 = (bf16[400,768]{1,0:T(8,128)(2,1)}, bf16[400,768]{1,0:T(8,128)(2,1)}, bf16[400,768]{1,0:T(8,128)(2,1)}, bf16[400,768]{1,0:T(8,128)(2,1)}) custom-call(bf16[2,256,768]{2,1,0:T(8,128)(2,1)} %get-tuple-element.156.xka, bf16[2,256,768]{2,1,0:T(8,128)(2,1)} %collective-permute-done.32.xra, bf16[528,768]{1,0:T(8,128)(2,1)} %get-tuple-element.158.dka, ...), custom_call_target="tpu_custom_call" | custom-call | flops 1000 | bytes 1024 | tf_op jit(solution)/shard_map/attention_weights_0/pallas_call | solution.py:616
  273.8 8.6 %collective-permute-done.45 = bf16[384,768]{1,0:T(8,128)(2,1)S(1)} collective-permute-done((bf16[384,768]{1,0:T(8,128)(2,1)}, bf16[384,768]{1,0:T(8,128)(2,1)S(1)}, u32[]{:S(2)}, u32[]{:S(2)}) %collective-permute-start.45) | collective-permute-done | bytes 589856 | tf_op jit(solution)/shard_map/ppermute | solution.py:31
  283.5 2.6 collective-permute-start.36
  286.5 5.3 %collective-permute-done.39 = bf16[384,768]{1,0:T(8,128)(2,1)S(1)} collective-permute-done((bf16[384,768]{1,0:T(8,128)(2,1)S(1)}, bf16[384,768]{1,0:T(8,128)(2,1)S(1)}, u32[]{:S(2)}, u32[]{:S(2)}) %collective-permute-start.39) | collective-permute-done | bytes 589856 | tf_op jit(solution)/shard_map/ppermute | solution.py:31
  291.8 6.4 %collective-permute-done.40 = bf16[384,768]{1,0:T(8,128)(2,1)S(1)} collective-permute-done((bf16[384,768]{1,0:T(8,128)(2,1)S(1)}, bf16[384,768]{1,0:T(8,128)(2,1)S(1)}, u32[]{:S(2)}, u32[]{:S(2)}) %collective-permute-start.40) | collective-permute-done | bytes 589856 | tf_op jit(solution)/shard_map/ppermute | solution.py:31
  298.3 1.9 collective-permute-start.48
  301.9 11.5 %collective-permute-done.36 = bf16[400,768]{1,0:T(8,128)(2,1)S(1)} collective-permute-done((bf16[400,768]{1,0:T(8,128)(2,1)}, bf16[400,768]{1,0:T(8,128)(2,1)S(1)}, u32[]{:S(2)}, u32[]{:S(2)}) %collective-permute-start.36) | collective-permute-done | bytes 614432 | tf_op jit(solution)/shard_map/ppermute | solution.py:31
  313.4 2.7 collective-permute-done.37
  317.9 2.0 collective-permute-start.43
  320.8 3.9 %collective-permute-done.48 = bf16[96,768]{1,0:T(8,128)(2,1)S(1)} collective-permute-done((bf16[96,768]{1,0:T(8,128)(2,1)S(1)}, bf16[96,768]{1,0:T(8,128)(2,1)S(1)}, u32[]{:S(2)}, u32[]{:S(2)}) %collective-permute-start.48) | collective-permute-done | bytes 147488 | tf_op jit(solution)/shard_map/ppermute | solution.py:31
  325.3 5.5 %collective-permute-done.42 = bf16[208,768]{1,0:T(8,128)(2,1)S(1)} collective-permute-done((bf16[208,768]{1,0:T(8,128)(2,1)S(1)}, bf16[208,768]{1,0:T(8,128)(2,1)S(1)}, u32[]{:S(2)}, u32[]{:S(2)}) %collective-permute-start.42) | collective-permute-done | bytes 319520 | tf_op jit(solution)/shard_map/ppermute | solution.py:31
  330.8 3.1 collective-permute-done.43
  335.8 3.7 collective-permute-start.54
  339.9 2.5 collective-permute-start.52
  342.5 2.7 collective-permute-done.50
  347.5 2.7 collective-permute-start.56
  350.3 3.0 collective-permute-start.57
  354.5 3.3 collective-permute-done.57
  358.6 5.2 %collective-permute-start.62 = (f32[24,768]{1,0:T(8,128)S(1)}, f32[24,768]{1,0:T(8,128)S(1)}, u32[]{:S(2)}, u32[]{:S(2)}) collective-permute-start(f32[24,768]{1,0:T(8,128)S(1)} %slice_bitcast_fusion.11), channel_id=1, source_target_pairs={{0,0},{1,32},{32,1},{33,33},{64,64},{65,96},{96,65},{97,97},{2,2},... | collective-permute-start | bytes 221192 | tf_op jit(solution)/shard_map/ppermute | solution.py:887
  (293 shorter events, 69.1 us)
Async XLA Ops:
  7.2 62.2 %all-gather.5.cloned.1.call-start = ((), (), s32[]{:S(2)}) async-start(), calls=%async_computation.2 | async-start | bytes 1474560 | tf_op jit(solution)/shard_map/all_gather | solution.py:764
  13.8 14.3 %collective-permute-start.3 = (bf16[104,768]{1,0:T(8,128)(2,1)}, bf16[104,768]{1,0:T(8,128)(2,1)S(1)}, u32[]{:S(2)}, u32[]{:S(2)}) collective-permute-start(bf16[104,768]{1,0:T(8,128)(2,1)} %get-tuple-element.102), channel_id=1, source_target_pairs={{0,2},{2,4},{4,6},{6,0},{1,3},{3,5},{5,7},{7,1},{8,10},{10,12},{12... | collective-permute-start | bytes 479240 | tf_op jit(solution)/shard_map/ppermute | solution.py:31
  15.9 12.3 %collective-permute-start.4 = (bf16[104,768]{1,0:T(8,128)(2,1)}, bf16[104,768]{1,0:T(8,128)(2,1)S(1)}, u32[]{:S(2)}, u32[]{:S(2)}) collective-permute-start(bf16[104,768]{1,0:T(8,128)(2,1)} %get-tuple-element.102), channel_id=1, source_target_pairs={{0,4},{2,6},{4,0},{6,2},{1,5},{3,7},{5,1},{7,3},{8,12},{10,14},{12... | collective-permute-start | bytes 479240 | tf_op jit(solution)/shard_map/ppermute | solution.py:31
  18.3 9.9 %collective-permute-start.5 = (bf16[104,768]{1,0:T(8,128)(2,1)}, bf16[104,768]{1,0:T(8,128)(2,1)S(1)}, u32[]{:S(2)}, u32[]{:S(2)}) collective-permute-start(bf16[104,768]{1,0:T(8,128)(2,1)} %get-tuple-element.102), channel_id=1, source_target_pairs={{0,6},{2,0},{4,2},{6,4},{1,7},{3,1},{5,3},{7,5},{8,14},{10,8},{12,... | collective-permute-start | bytes 479240 | tf_op jit(solution)/shard_map/ppermute | solution.py:31
  36.0 85.0 %all-gather.7.cloned.1.call-start = ((), (), s32[]{:S(2)}) async-start(), calls=%async_computation.3 | async-start | bytes 5898240 | tf_op jit(solution)/shard_map/all_gather | solution.py:774
  39.0 16.0 %collective-permute-start.7 = (bf16[400,768]{1,0:T(8,128)(2,1)S(1)}, bf16[400,768]{1,0:T(8,128)(2,1)S(1)}, u32[]{:S(2)}, u32[]{:S(2)}) collective-permute-start(bf16[400,768]{1,0:T(8,128)(2,1)S(1)} %maximum_maximum_fusion), channel_id=1, source_target_pairs={{0,64},{1,9},{8,72},{9,17},{16,80},{17,25},{24,88},{25,1},{64,32},... | collective-permute-start | bytes 1843208 | tf_op jit(solution)/shard_map/ppermute | solution.py:55
  40.7 27.0 %collective-permute-start.8 = (bf16[400,768]{1,0:T(8,128)(2,1)S(1)}, bf16[400,768]{1,0:T(8,128)(2,1)S(1)}, u32[]{:S(2)}, u32[]{:S(2)}) collective-permute-start(bf16[400,768]{1,0:T(8,128)(2,1)S(1)} %maximum_maximum_fusion), channel_id=1, source_target_pairs={{0,32},{1,17},{8,40},{9,25},{16,48},{17,1},{24,56},{25,9},{64,96},... | collective-permute-start | bytes 1843208 | tf_op jit(solution)/shard_map/ppermute | solution.py:55
  44.0 23.7 %collective-permute-start.9 = (bf16[400,768]{1,0:T(8,128)(2,1)S(1)}, bf16[400,768]{1,0:T(8,128)(2,1)S(1)}, u32[]{:S(2)}, u32[]{:S(2)}) collective-permute-start(bf16[400,768]{1,0:T(8,128)(2,1)S(1)} %maximum_maximum_fusion), channel_id=1, source_target_pairs={{0,96},{1,25},{8,104},{9,1},{16,112},{17,9},{24,120},{25,17},{64,0... | collective-permute-start | bytes 1843208 | tf_op jit(solution)/shard_map/ppermute | solution.py:55
  69.4 276.7 %reduce-scatter.2.cloned.1.call-start = ((), (), s32[]{:S(2)}) async-start(), calls=%async_computation.1 | async-start | bytes 7938048 | tf_op jit(solution)/shard_map/reduce_scatter | solution.py:927
  71.3 17.2 %collective-permute-start.10 = (bf16[2,400,768]{2,1,0:T(8,128)(2,1)S(1)}, bf16[2,400,768]{2,1,0:T(8,128)(2,1)S(1)}, u32[]{:S(2)}, u32[]{:S(2)}) collective-permute-start(bf16[2,400,768]{2,1,0:T(8,128)(2,1)S(1)} %get-tuple-element.215.refs_3_.refs_2_.refs_5_.refs_7_), channel_id=1, source_target_pairs={{0,8},{1,65},{8,16},{9,73},{16,24},{17,81},{24,0},{25,89},{64,72},... | collective-permute-start | bytes 3686408 | tf_op jit(solution)/shard_map/ppermute | solution.py:55
  71.3 31.7 %collective-permute-start.11 = (bf16[2,400,768]{2,1,0:T(8,128)(2,1)S(1)}, bf16[2,400,768]{2,1,0:T(8,128)(2,1)}, u32[]{:S(2)}, u32[]{:S(2)}) collective-permute-start(bf16[2,400,768]{2,1,0:T(8,128)(2,1)S(1)} %get-tuple-element.215.refs_3_.refs_2_.refs_5_.refs_7_), channel_id=1, source_target_pairs={{0,16},{1,33},{8,24},{9,41},{16,0},{17,49},{24,8},{25,57},{64,80},... | collective-permute-start | bytes 3686408 | tf_op jit(solution)/shard_map/ppermute | solution.py:55
  74.1 29.0 %collective-permute-start.12 = (bf16[2,400,768]{2,1,0:T(8,128)(2,1)S(1)}, bf16[2,400,768]{2,1,0:T(8,128)(2,1)}, u32[]{:S(2)}, u32[]{:S(2)}) collective-permute-start(bf16[2,400,768]{2,1,0:T(8,128)(2,1)S(1)} %get-tuple-element.215.refs_3_.refs_2_.refs_5_.refs_7_), channel_id=1, source_target_pairs={{0,24},{1,97},{8,0},{9,105},{16,8},{17,113},{24,16},{25,121},{64,8... | collective-permute-start | bytes 3686408 | tf_op jit(solution)/shard_map/ppermute | solution.py:55
  74.3 31.3 %collective-permute-start.13 = (bf16[2,400,768]{2,1,0:T(8,128)(2,1)S(1)}, bf16[2,400,768]{2,1,0:T(8,128)(2,1)}, u32[]{:S(2)}, u32[]{:S(2)}) collective-permute-start(bf16[2,400,768]{2,1,0:T(8,128)(2,1)S(1)} %get-tuple-element.215.refs_3_.refs_2_.refs_5_.refs_7_), channel_id=1, source_target_pairs={{0,1},{1,0},{2,3},{3,2},{4,5},{5,4},{6,7},{7,6},{8,9},{9,8},{10,11... | collective-permute-start | bytes 3686408 | tf_op jit(solution)/shard_map/ppermute | solution.py:31
  88.5 18.0 %collective-permute-start.14 = (bf16[2,400,768]{2,1,0:T(8,128)(2,1)S(1)}, bf16[2,400,768]{2,1,0:T(8,128)(2,1)}, u32[]{:S(2)}, u32[]{:S(2)}) collective-permute-start(bf16[2,400,768]{2,1,0:T(8,128)(2,1)S(1)} %collective-permute-done.10.refs_4_.refs_3_.refs_6_.refs_8_), channel_id=1, source_target_pairs={{0,1},{1,0},{2,3},{3,2},{4,5},{5,4},{6,7},{7,6},{8,9},{9,8},{10,11... | collective-permute-start | bytes 3686408 | tf_op jit(solution)/shard_map/ppermute | solution.py:31
  120.9 31.3 %collective-permute-start.20 = (bf16[4,4,4,48,768]{4,3,2,1,0:T(8,128)(2,1)}, bf16[4,4,4,48,768]{4,3,2,1,0:T(8,128)(2,1)S(1)}, u32[]{:S(2)}, u32[]{:S(2)}) collective-permute-start(bf16[4,4,4,48,768]{4,3,2,1,0:T(8,128)(2,1)} %bitcast.225), channel_id=1, source_target_pairs={{0,1},{1,0},{2,3},{3,2},{4,5},{5,4},{6,7},{7,6},{8,9},{9,8},{10,11... | collective-permute-start | bytes 14155784 | tf_op jit(solution)/shard_map/ppermute | solution.py:31
  121.4 17.1 %collective-permute-start.17 = (bf16[2,400,768]{2,1,0:T(8,128)(2,1)S(1)}, bf16[2,400,768]{2,1,0:T(8,128)(2,1)S(1)}, u32[]{:S(2)}, u32[]{:S(2)}) collective-permute-start(bf16[2,400,768]{2,1,0:T(8,128)(2,1)S(1)} %copy-done.3), channel_id=1, source_target_pairs={{0,8},{1,65},{8,16},{9,73},{16,24},{17,81},{24,0},{25,89},{64,72},... | collective-permute-start | bytes 3686408 | tf_op jit(solution)/shard_map/ppermute | solution.py:55
  121.4 30.1 %collective-permute-start.18 = (bf16[2,400,768]{2,1,0:T(8,128)(2,1)S(1)}, bf16[2,400,768]{2,1,0:T(8,128)(2,1)S(1)}, u32[]{:S(2)}, u32[]{:S(2)}) collective-permute-start(bf16[2,400,768]{2,1,0:T(8,128)(2,1)S(1)} %copy-done.3), channel_id=1, source_target_pairs={{0,16},{1,33},{8,24},{9,41},{16,0},{17,49},{24,8},{25,57},{64,80},... | collective-permute-start | bytes 3686408 | tf_op jit(solution)/shard_map/ppermute | solution.py:55
  124.2 28.1 %collective-permute-start.19 = (bf16[2,400,768]{2,1,0:T(8,128)(2,1)S(1)}, bf16[2,400,768]{2,1,0:T(8,128)(2,1)S(1)}, u32[]{:S(2)}, u32[]{:S(2)}) collective-permute-start(bf16[2,400,768]{2,1,0:T(8,128)(2,1)S(1)} %copy-done.3), channel_id=1, source_target_pairs={{0,24},{1,97},{8,0},{9,105},{16,8},{17,113},{24,16},{25,121},{64,8... | collective-permute-start | bytes 3686408 | tf_op jit(solution)/shard_map/ppermute | solution.py:55
  124.6 27.7 %collective-permute-start.21 = (bf16[2,400,768]{2,1,0:T(8,128)(2,1)S(1)}, bf16[2,400,768]{2,1,0:T(8,128)(2,1)S(1)}, u32[]{:S(2)}, u32[]{:S(2)}) collective-permute-start(bf16[2,400,768]{2,1,0:T(8,128)(2,1)S(1)} %copy-done.3), channel_id=1, source_target_pairs={{0,1},{1,0},{2,3},{3,2},{4,5},{5,4},{6,7},{7,6},{8,9},{9,8},{10,11... | collective-permute-start | bytes 3686408 | tf_op jit(solution)/shard_map/ppermute | solution.py:31
  195.8 12.6 %collective-permute-start.26 = (bf16[3,256,768]{2,1,0:T(8,128)(2,1)}, bf16[3,256,768]{2,1,0:T(8,128)(2,1)S(1)}, u32[]{:S(2)}, u32[]{:S(2)}) collective-permute-start(bf16[3,256,768]{2,1,0:T(8,128)(2,1)} %get-tuple-element.132), channel_id=1, source_target_pairs={{0,1},{1,0},{2,3},{3,2},{4,5},{5,4},{6,7},{7,6},{8,9},{9,8},{10,11... | collective-permute-start | bytes 3538952 | tf_op jit(solution)/shard_map/ppermute | solution.py:31
  196.3 12.1 %collective-permute-start.27 = (bf16[3,256,768]{2,1,0:T(8,128)(2,1)}, bf16[3,256,768]{2,1,0:T(8,128)(2,1)S(1)}, u32[]{:S(2)}, u32[]{:S(2)}) collective-permute-start(bf16[3,256,768]{2,1,0:T(8,128)(2,1)} %get-tuple-element.133), channel_id=1, source_target_pairs={{0,1},{1,0},{2,3},{3,2},{4,5},{5,4},{6,7},{7,6},{8,9},{9,8},{10,11... | collective-permute-start | bytes 3538952 | tf_op jit(solution)/shard_map/ppermute | solution.py:31
  196.4 12.0 %collective-permute-start.29 = (bf16[528,768]{1,0:T(8,128)(2,1)}, bf16[528,768]{1,0:T(8,128)(2,1)S(1)}, u32[]{:S(2)}, u32[]{:S(2)}) collective-permute-start(bf16[528,768]{1,0:T(8,128)(2,1)} %get-tuple-element.135), channel_id=1, source_target_pairs={{0,1},{1,0},{2,3},{3,2},{4,5},{5,4},{6,7},{7,6},{8,9},{9,8},{10,11... | collective-permute-start | bytes 2433032 | tf_op jit(solution)/shard_map/ppermute | solution.py:31
  196.8 11.5 %collective-permute-start.28 = (bf16[2,256,768]{2,1,0:T(8,128)(2,1)}, bf16[2,256,768]{2,1,0:T(8,128)(2,1)S(1)}, u32[]{:S(2)}, u32[]{:S(2)}) collective-permute-start(bf16[2,256,768]{2,1,0:T(8,128)(2,1)} %get-tuple-element.134), channel_id=1, source_target_pairs={{0,1},{1,0},{2,3},{3,2},{4,5},{5,4},{6,7},{7,6},{8,9},{9,8},{10,11... | collective-permute-start | bytes 2359304 | tf_op jit(solution)/shard_map/ppermute | solution.py:31
  218.3 16.7 %collective-permute-start.31 = (bf16[3,256,768]{2,1,0:T(8,128)(2,1)}, bf16[3,256,768]{2,1,0:T(8,128)(2,1)S(1)}, u32[]{:S(2)}, u32[]{:S(2)}) collective-permute-start(bf16[3,256,768]{2,1,0:T(8,128)(2,1)} %get-tuple-element.153), channel_id=1, source_target_pairs={{0,1},{1,0},{2,3},{3,2},{4,5},{5,4},{6,7},{7,6},{8,9},{9,8},{10,11... | collective-permute-start | bytes 3538952 | tf_op jit(solution)/shard_map/ppermute | solution.py:31
  218.8 16.2 %collective-permute-start.30 = (bf16[3,256,768]{2,1,0:T(8,128)(2,1)}, bf16[3,256,768]{2,1,0:T(8,128)(2,1)S(1)}, u32[]{:S(2)}, u32[]{:S(2)}) collective-permute-start(bf16[3,256,768]{2,1,0:T(8,128)(2,1)} %get-tuple-element.152), channel_id=1, source_target_pairs={{0,1},{1,0},{2,3},{3,2},{4,5},{5,4},{6,7},{7,6},{8,9},{9,8},{10,11... | collective-permute-start | bytes 3538952 | tf_op jit(solution)/shard_map/ppermute | solution.py:31
  231.1 12.9 %collective-permute-start.34 = (bf16[528,768]{1,0:T(8,128)(2,1)}, bf16[528,768]{1,0:T(8,128)(2,1)}, u32[]{:S(2)}, u32[]{:S(2)}) collective-permute-start(bf16[528,768]{1,0:T(8,128)(2,1)} %get-tuple-element.171), channel_id=1, source_target_pairs={{0,1},{1,0},{2,3},{3,2},{4,5},{5,4},{6,7},{7,6},{8,9},{9,8},{10,11... | collective-permute-start | bytes 2433032 | tf_op jit(solution)/shard_map/ppermute | solution.py:31
  232.5 15.8 %collective-permute-start.25 = (bf16[256,768]{1,0:T(8,128)(2,1)}, bf16[256,768]{1,0:T(8,128)(2,1)S(1)}, u32[]{:S(2)}, u32[]{:S(2)}) collective-permute-start(bf16[256,768]{1,0:T(8,128)(2,1)} %broadcast_select_fusion.6), channel_id=1, source_target_pairs={{0,64},{64,0},{1,65},{65,1},{2,66},{66,2},{3,67},{67,3},{4,68},{68... | collective-permute-start | bytes 1179656 | tf_op jit(solution)/shard_map/ppermute | solution.py:31
  244.0 23.4 %collective-permute-start.44 = (bf16[384,768]{1,0:T(8,128)(2,1)}, bf16[384,768]{1,0:T(8,128)(2,1)S(1)}, u32[]{:S(2)}, u32[]{:S(2)}) collective-permute-start(bf16[384,768]{1,0:T(8,128)(2,1)} %get-tuple-element.182), channel_id=1, source_target_pairs={{0,64},{64,32},{32,96},{96,0},{1,65},{65,33},{33,97},{97,1},{2,66}... | collective-permute-start | bytes 1769480 | tf_op jit(solution)/shard_map/ppermute | solution.py:31
  244.4 21.2 %collective-permute-start.33 = (bf16[256,768]{1,0:T(8,128)(2,1)S(1)}, bf16[256,768]{1,0:T(8,128)(2,1)S(1)}, u32[]{:S(2)}, u32[]{:S(2)}) collective-permute-start(bf16[256,768]{1,0:T(8,128)(2,1)S(1)} %broadcast_select_fusion.2), channel_id=1, source_target_pairs={{0,64},{64,0},{1,65},{65,1},{2,66},{66,2},{3,67},{67,3},{4,68},{68... | collective-permute-start | bytes 1179656 | tf_op jit(solution)/shard_map/ppermute | solution.py:31
  245.1 37.2 %collective-permute-start.45 = (bf16[384,768]{1,0:T(8,128)(2,1)}, bf16[384,768]{1,0:T(8,128)(2,1)S(1)}, u32[]{:S(2)}, u32[]{:S(2)}) collective-permute-start(bf16[384,768]{1,0:T(8,128)(2,1)} %get-tuple-element.183), channel_id=1, source_target_pairs={{0,32},{64,96},{32,0},{96,64},{1,33},{65,97},{33,1},{97,65},{2,34}... | collective-permute-start | bytes 1769480 | tf_op jit(solution)/shard_map/ppermute | solution.py:31
  248.1 35.4 %collective-permute-start.46 = (bf16[384,768]{1,0:T(8,128)(2,1)}, bf16[384,768]{1,0:T(8,128)(2,1)S(1)}, u32[]{:S(2)}, u32[]{:S(2)}) collective-permute-start(bf16[384,768]{1,0:T(8,128)(2,1)} %get-tuple-element.184), channel_id=1, source_target_pairs={{0,96},{64,0},{32,64},{96,32},{1,97},{65,1},{33,65},{97,33},{2,98}... | collective-permute-start | bytes 1769480 | tf_op jit(solution)/shard_map/ppermute | solution.py:31
  248.4 37.9 %collective-permute-start.38 = (bf16[384,768]{1,0:T(8,128)(2,1)S(1)}, bf16[384,768]{1,0:T(8,128)(2,1)S(1)}, u32[]{:S(2)}, u32[]{:S(2)}) collective-permute-start(bf16[384,768]{1,0:T(8,128)(2,1)S(1)} %copy-done.34), channel_id=1, source_target_pairs={{0,2},{2,4},{4,6},{6,0},{1,3},{3,5},{5,7},{7,1},{8,10},{10,12},{12... | collective-permute-start | bytes 1769480 | tf_op jit(solution)/shard_map/ppermute | solution.py:31
  265.6 26.2 %collective-permute-start.39 = (bf16[384,768]{1,0:T(8,128)(2,1)S(1)}, bf16[384,768]{1,0:T(8,128)(2,1)S(1)}, u32[]{:S(2)}, u32[]{:S(2)}) collective-permute-start(bf16[384,768]{1,0:T(8,128)(2,1)S(1)} %copy-done.33), channel_id=1, source_target_pairs={{0,4},{2,6},{4,0},{6,2},{1,5},{3,7},{5,1},{7,3},{8,12},{10,14},{12... | collective-permute-start | bytes 1769480 | tf_op jit(solution)/shard_map/ppermute | solution.py:31
  267.4 30.8 %collective-permute-start.40 = (bf16[384,768]{1,0:T(8,128)(2,1)S(1)}, bf16[384,768]{1,0:T(8,128)(2,1)S(1)}, u32[]{:S(2)}, u32[]{:S(2)}) collective-permute-start(bf16[384,768]{1,0:T(8,128)(2,1)S(1)} %copy-done.32), channel_id=1, source_target_pairs={{0,6},{2,0},{4,2},{6,4},{1,7},{3,1},{5,3},{7,5},{8,14},{10,8},{12,... | collective-permute-start | bytes 1769480 | tf_op jit(solution)/shard_map/ppermute | solution.py:31
  282.4 18.2 %collective-permute-start.35 = (bf16[400,768]{1,0:T(8,128)(2,1)}, bf16[400,768]{1,0:T(8,128)(2,1)S(1)}, u32[]{:S(2)}, u32[]{:S(2)}) collective-permute-start(bf16[400,768]{1,0:T(8,128)(2,1)} %get-tuple-element.174), channel_id=1, source_target_pairs={{0,8},{8,16},{16,24},{24,0},{1,9},{9,17},{17,25},{25,1},{2,10},{10... | collective-permute-start | bytes 1843208 | tf_op jit(solution)/shard_map/ppermute | solution.py:31
  283.5 30.0 %collective-permute-start.36 = (bf16[400,768]{1,0:T(8,128)(2,1)}, bf16[400,768]{1,0:T(8,128)(2,1)S(1)}, u32[]{:S(2)}, u32[]{:S(2)}) collective-permute-start(bf16[400,768]{1,0:T(8,128)(2,1)} %get-tuple-element.175), channel_id=1, source_target_pairs={{0,16},{8,24},{16,0},{24,8},{1,17},{9,25},{17,1},{25,9},{2,18},{10... | collective-permute-start | bytes 1843208 | tf_op jit(solution)/shard_map/ppermute | solution.py:31
  286.3 29.8 %collective-permute-start.37 = (bf16[400,768]{1,0:T(8,128)(2,1)S(1)}, bf16[400,768]{1,0:T(8,128)(2,1)S(1)}, u32[]{:S(2)}, u32[]{:S(2)}) collective-permute-start(bf16[400,768]{1,0:T(8,128)(2,1)S(1)} %copy-done.31), channel_id=1, source_target_pairs={{0,24},{8,0},{16,8},{24,16},{1,25},{9,1},{17,9},{25,17},{2,26},{10... | collective-permute-start | bytes 1843208 | tf_op jit(solution)/shard_map/ppermute | solution.py:31
  291.8 26.1 %collective-permute-start.47 = (bf16[96,768]{1,0:T(8,128)(2,1)S(1)}, bf16[96,768]{1,0:T(8,128)(2,1)S(1)}, u32[]{:S(2)}, u32[]{:S(2)}) collective-permute-start(bf16[96,768]{1,0:T(8,128)(2,1)S(1)} %get-tuple-element.225), channel_id=1, source_target_pairs={{0,8},{8,16},{16,24},{24,0},{1,9},{9,17},{17,25},{25,1},{2,10},{10... | collective-permute-start | bytes 442376 | tf_op jit(solution)/shard_map/ppermute | solution.py:31
  298.3 26.5 %collective-permute-start.48 = (bf16[96,768]{1,0:T(8,128)(2,1)S(1)}, bf16[96,768]{1,0:T(8,128)(2,1)S(1)}, u32[]{:S(2)}, u32[]{:S(2)}) collective-permute-start(bf16[96,768]{1,0:T(8,128)(2,1)S(1)} %get-tuple-element.227), channel_id=1, source_target_pairs={{0,16},{8,24},{16,0},{24,8},{1,17},{9,25},{17,1},{25,9},{2,18},{10... | collective-permute-start | bytes 442376 | tf_op jit(solution)/shard_map/ppermute | solution.py:31
  300.6 24.4 %collective-permute-start.49 = (bf16[96,768]{1,0:T(8,128)(2,1)S(1)}, bf16[96,768]{1,0:T(8,128)(2,1)S(1)}, u32[]{:S(2)}, u32[]{:S(2)}) collective-permute-start(bf16[96,768]{1,0:T(8,128)(2,1)S(1)} %get-tuple-element.226), channel_id=1, source_target_pairs={{0,24},{8,0},{16,8},{24,16},{1,25},{9,1},{17,9},{25,17},{2,26},{10... | collective-permute-start | bytes 442376 | tf_op jit(solution)/shard_map/ppermute | solution.py:31
  316.9 8.3 %collective-permute-start.41 = (bf16[208,768]{1,0:T(8,128)(2,1)S(1)}, bf16[208,768]{1,0:T(8,128)(2,1)S(1)}, u32[]{:S(2)}, u32[]{:S(2)}) collective-permute-start(bf16[208,768]{1,0:T(8,128)(2,1)S(1)} %get-tuple-element.216), channel_id=1, source_target_pairs={{0,64},{64,32},{32,96},{96,0},{1,65},{65,33},{33,97},{97,1},{2,66}... | collective-permute-start | bytes 958472 | tf_op jit(solution)/shard_map/ppermute | solution.py:31
  317.0 13.8 %collective-permute-start.42 = (bf16[208,768]{1,0:T(8,128)(2,1)S(1)}, bf16[208,768]{1,0:T(8,128)(2,1)S(1)}, u32[]{:S(2)}, u32[]{:S(2)}) collective-permute-start(bf16[208,768]{1,0:T(8,128)(2,1)S(1)} %get-tuple-element.218), channel_id=1, source_target_pairs={{0,32},{64,96},{32,0},{96,64},{1,33},{65,97},{33,1},{97,65},{2,34}... | collective-permute-start | bytes 958472 | tf_op jit(solution)/shard_map/ppermute | solution.py:31
  317.9 16.0 %collective-permute-start.43 = (bf16[208,768]{1,0:T(8,128)(2,1)S(1)}, bf16[208,768]{1,0:T(8,128)(2,1)S(1)}, u32[]{:S(2)}, u32[]{:S(2)}) collective-permute-start(bf16[208,768]{1,0:T(8,128)(2,1)S(1)} %get-tuple-element.217), channel_id=1, source_target_pairs={{0,96},{64,0},{32,64},{96,32},{1,97},{65,1},{33,65},{97,33},{2,98}... | collective-permute-start | bytes 958472 | tf_op jit(solution)/shard_map/ppermute | solution.py:31
  335.8 6.6 %collective-permute-start.54 = (bf16[24,768]{1,0:T(8,128)(2,1)S(1)}, bf16[24,768]{1,0:T(8,128)(2,1)S(1)}, u32[]{:S(2)}, u32[]{:S(2)}) collective-permute-start(bf16[24,768]{1,0:T(8,128)(2,1)S(1)} %get-tuple-element.272), channel_id=1, source_target_pairs={{0,16},{8,24},{16,0},{24,8},{1,17},{9,25},{17,1},{25,9},{2,18},{10... | collective-permute-start | bytes 110600 | tf_op jit(solution)/shard_map/ppermute | solution.py:31
  347.5 7.0 %collective-permute-start.56 = (bf16[88,768]{1,0:T(8,128)(2,1)S(1)}, bf16[88,768]{1,0:T(8,128)(2,1)S(1)}, u32[]{:S(2)}, u32[]{:S(2)}) collective-permute-start(bf16[88,768]{1,0:T(8,128)(2,1)S(1)} %get-tuple-element.236), channel_id=1, source_target_pairs={{0,64},{64,32},{32,96},{96,0},{1,65},{65,33},{33,97},{97,1},{2,66}... | collective-permute-start | bytes 405512 | tf_op jit(solution)/shard_map/ppermute | solution.py:31
  350.3 7.6 %collective-permute-start.57 = (bf16[88,768]{1,0:T(8,128)(2,1)S(1)}, bf16[88,768]{1,0:T(8,128)(2,1)S(1)}, u32[]{:S(2)}, u32[]{:S(2)}) collective-permute-start(bf16[88,768]{1,0:T(8,128)(2,1)S(1)} %get-tuple-element.238), channel_id=1, source_target_pairs={{0,32},{64,96},{32,0},{96,64},{1,33},{65,97},{33,1},{97,65},{2,34}... | collective-permute-start | bytes 405512 | tf_op jit(solution)/shard_map/ppermute | solution.py:31
  358.6 14.9 %collective-permute-start.62 = (f32[24,768]{1,0:T(8,128)S(1)}, f32[24,768]{1,0:T(8,128)S(1)}, u32[]{:S(2)}, u32[]{:S(2)}) collective-permute-start(f32[24,768]{1,0:T(8,128)S(1)} %slice_bitcast_fusion.11), channel_id=1, source_target_pairs={{0,0},{1,32},{32,1},{33,33},{64,64},{65,96},{96,65},{97,97},{2,2},... | collective-permute-start | bytes 221192 | tf_op jit(solution)/shard_map/ppermute | solution.py:887
  363.9 9.7 %collective-permute-start.63 = (f32[24,768]{1,0:T(8,128)S(1)}, f32[24,768]{1,0:T(8,128)S(1)}, u32[]{:S(2)}, u32[]{:S(2)}) collective-permute-start(f32[24,768]{1,0:T(8,128)S(1)} %slice_bitcast_fusion.10), channel_id=1, source_target_pairs={{0,64},{1,96},{32,65},{33,97},{64,0},{65,32},{96,1},{97,33},{2,66}... | collective-permute-start | bytes 221192 | tf_op jit(solution)/shard_map/ppermute | solution.py:887
  (55 other events, 561.8 us)
Sparse Core Ops, SparseCore 0:
  36.1 33.2 all-gather.4
  71.1 47.6 all-gather.6
  218.4 111.6 reduce-scatter.1
